TPU v7x, 256 devices: a whole 4x4x8 slice. The times are simulated.
256 devices in a mesh: row: 16 (over x_lo, y, core), col: 8 (over z), rep: 2 (over x_hi).
Axes of the slice: x: 4 (x_hi: 2, x_lo: 2; x = x_hi * 2 + x_lo), y: 4, z: 8, core: 2. Of those that a mesh axis runs over, the one named last changes fastest.
Arguments:
- pair: bfloat16 [1024, 512, 128], P(('rep', 'row'), 'col'), parts along dimension 0, may hold values from -6 to 6
- pad_mask: int32 [1024], P('rep'), parts along dimension 0, may hold values 0 or 1
- crop_mask: int32 [1024], P('rep'), parts along dimension 0, may hold values 0 or 1
- left_proj: bfloat16 [128, 128], replicated, may hold values from -0.5 to 0.5
- left_gate: bfloat16 [128, 128], replicated, may hold values from -0.5 to 0.5
- right_proj: bfloat16 [128, 128], replicated, may hold values from -0.5 to 0.5
- right_gate: bfloat16 [128, 128], replicated, may hold values from -0.5 to 0.5
- out_gate: bfloat16 [128, 128], replicated, may hold values from -0.5 to 0.5
- out_proj: bfloat16 [128, 128], replicated, may hold values from -0.5 to 0.5
- cotangent: bfloat16 [1024, 512, 128], P(('rep', 'row'), 'col'), parts along dimension 0, may hold values from -6 to 6
Outputs:
- result: bfloat16 [1024, 512, 128], P(('rep', 'row'), 'col'), parts along dimension 0
- grad_pair: bfloat16 [1024, 512, 128], P(('rep', 'row'), 'col'), parts along dimension 0
- weight_grads: float32 [12, 128, 128], P('rep'), parts along dimension 0
There are 2 independent parts, one for each index of `rep`. A program takes and returns all parts, laid end to end along the dimension named above; an argument that names none is the same for every part. Nothing has to cross between parts.
Inputs may be any that keep to these rules, and one draw needn't show every extreme that they name: pad_mask and crop_mask hold only 0 and 1.
All inputs are finite; a program needn't handle non-finite values.
Results may differ from a plain program's by a relative error of at most 0.025.
Values may be sent and summed in bfloat16 or wider, within the bound.
A program may use at most 128 MiB of HBM per device.

v0:
```python
import jax
import jax.numpy as jnp
from jax import lax
from jax.sharding import PartitionSpec as P


def layer_norm(values):
    center = values - jnp.mean(values, -1, keepdims=True)
    spread = jnp.mean(center * center, -1, keepdims=True)
    return center * lax.rsqrt(spread + 1e-05)


def project(source, weight):
    return jnp.einsum("ijc,cd->ijd", source, weight, preferred_element_type=jnp.float32)


def back_project(source, weight):
    return jnp.einsum("ijd,cd->ijc", source, weight, preferred_element_type=jnp.float32)


def outer_sum(left, right):
    return jnp.einsum("ijc,ijd->cd", left, right, preferred_element_type=jnp.float32)


def shards(
    pair,
    pad_mask,
    crop_mask,
    left_proj,
    left_gate,
    right_proj,
    right_gate,
    out_gate,
    out_proj,
    cotangent,
):
    row_count = pair.shape[0]
    col_count = pair.shape[1]
    row_devices = lax.axis_size("row")
    total = row_count * row_devices
    row_start = lax.axis_index("row") * row_count
    col_start = lax.axis_index("col") * col_count
    pad_float = pad_mask.astype(jnp.float32)
    crop_float = crop_mask.astype(jnp.float32)
    pad_rows = lax.dynamic_slice_in_dim(pad_float, row_start, row_count)
    pad_cols = lax.dynamic_slice_in_dim(pad_float, col_start, col_count)
    crop_rows = lax.dynamic_slice_in_dim(crop_float, row_start, row_count)
    crop_cols = lax.dynamic_slice_in_dim(crop_float, col_start, col_count)
    pair_mask = (pad_rows[:, None] * pad_cols[None, :])[:, :, None]
    crop_pair = (crop_rows[:, None] * crop_cols[None, :])[:, :, None]
    pair_float = pair.astype(jnp.float32)
    normed = layer_norm(pair_float).astype(jnp.bfloat16)
    left_value = project(normed, left_proj)
    left_sig = jax.nn.sigmoid(project(normed, left_gate))
    right_value = project(normed, right_proj)
    right_sig = jax.nn.sigmoid(project(normed, right_gate))
    left_edge = (pair_mask * left_sig * left_value).astype(jnp.bfloat16)
    right_edge = (pair_mask * right_sig * right_value).astype(jnp.bfloat16)
    right_panel = lax.all_gather(right_edge, "row", axis=0, tiled=True)
    gate_value = jax.nn.sigmoid(project(normed, out_gate))
    summed_cols = lax.psum_scatter(
        jnp.einsum(
            "jkc,ikc->jic", right_panel, left_edge, preferred_element_type=jnp.float32
        ).astype(jnp.bfloat16),
        "col",
        scatter_dimension=0,
        tiled=True,
    ).astype(jnp.float32)
    summed = jnp.transpose(summed_cols, (1, 0, 2))
    normed_sum = layer_norm(summed).astype(jnp.bfloat16)
    projected = project(normed_sum, out_proj)
    result = (crop_pair * gate_value * projected).astype(jnp.bfloat16)
    upstream = crop_pair * cotangent.astype(jnp.float32)
    grad_projected = (upstream * gate_value).astype(jnp.bfloat16)
    grad_gate_logit = (upstream * projected * gate_value * (1.0 - gate_value)).astype(jnp.bfloat16)
    grad_normed_sum = back_project(grad_projected, out_proj)
    _, sum_pullback = jax.vjp(layer_norm, summed)
    grad_summed = sum_pullback(grad_normed_sum)[0].astype(jnp.bfloat16)
    cotangent_panel = lax.all_gather(grad_summed, "col", axis=1, tiled=True)
    grad_left = jnp.einsum(
        "ijc,jkc->ikc", cotangent_panel, right_panel, preferred_element_type=jnp.float32
    )
    grad_right = lax.psum_scatter(
        jnp.einsum(
            "ijc,ikc->jkc", cotangent_panel, left_edge, preferred_element_type=jnp.float32
        ).astype(jnp.bfloat16),
        "row",
        scatter_dimension=0,
        tiled=True,
    ).astype(jnp.float32)
    grad_left_value = (grad_left * pair_mask * left_sig).astype(jnp.bfloat16)
    grad_left_logit = (grad_left * pair_mask * left_value * left_sig * (1.0 - left_sig)).astype(
        jnp.bfloat16
    )
    grad_right_value = (grad_right * pair_mask * right_sig).astype(jnp.bfloat16)
    grad_right_logit = (
        grad_right * pair_mask * right_value * right_sig * (1.0 - right_sig)
    ).astype(jnp.bfloat16)
    grad_normed = back_project(grad_left_value, left_proj) + back_project(
        grad_left_logit, left_gate
    )
    grad_normed = (
        grad_normed
        + back_project(grad_right_value, right_proj)
        + back_project(grad_right_logit, right_gate)
    )
    grad_normed = grad_normed + back_project(grad_gate_logit, out_gate)
    _, pair_pullback = jax.vjp(layer_norm, pair_float)
    grad_pair = pair_pullback(grad_normed)[0].astype(jnp.bfloat16)
    local_grads = jnp.stack(
        [
            outer_sum(normed, grad_left_value),
            outer_sum(normed, grad_left_logit),
            outer_sum(normed, grad_right_value),
            outer_sum(normed, grad_right_logit),
            outer_sum(normed, grad_gate_logit),
            outer_sum(normed_sum, grad_projected),
        ]
    ) / jnp.float32(total)
    weight_grads = lax.psum(local_grads, ("row", "col"))
    return (result, grad_pair, weight_grads)


def solution(mesh):
    return jax.shard_map(
        shards,
        mesh=mesh,
        in_specs=(
            P(("rep", "row"), "col", None),
            P("rep"),
            P("rep"),
            P(),
            P(),
            P(),
            P(),
            P(),
            P(),
            P(("rep", "row"), "col", None),
        ),
        out_specs=(
            P(("rep", "row"), "col", None),
            P(("rep", "row"), "col", None),
            P("rep", None, None),
        ),
        check_vma=False,
    )
```

profile of v0, /device:TPU:1, one launch (start us, length us, event | category | flops | bytes accessed | tf_op | source)
XLA Modules:
  0.0 1337.5 jit_solution(6953164047988596814)
XLA Ops:
  7.3 0.7 convert_element_type.70
  8.1 1.4 convert_reduce_fusion
  9.5 1.7 fusion.19
  11.3 1.9 fusion.6
  13.3 0.9 fusion.46
  14.3 1.4 fusion.8
  15.7 0.9 copy-done.5
  16.6 2.0 multiply_convert_fusion.7
  18.7 1.6 copy.23
  20.3 57.3 %all-gather.3.cloned.1.call-done = bf16[512,64,128]{2,1,0:T(8,128)(2,1)} async-done(((bf16[32,64,128]{2,1,0:T(8,128)(2,1)}), bf16[512,64,128]{2,1,0:T(8,128)(2,1)}) %all-gather.3.cloned.1.call-update) | async-done | bytes 8388624 | tf_op jit(solution)/shard_map/all_gather | solution.py:59
  77.6 23.7 %copy.24 = bf16[512,64,128]{1,0,2:T(8,128)(2,1)} copy(bf16[512,64,128]{2,1,0:T(8,128)(2,1)} %all-gather.3.cloned.1.call-done) | data formatting | bytes 16777216 | tf_op jit(solution)/shard_map/all_gather | solution.py:59
  101.4 10.5 convert_bitcast_fusion.1
  111.9 9.1 copy.25
  121.1 0.6 copy-done.15
  122.1 1.9 multiply_convert_fusion.5
  123.9 53.2 %reduce-scatter.3.cloned.1.call-done = bf16[64,32,128]{2,1,0:T(8,128)(2,1)} async-done(((bf16[512,32,128]{2,1,0:T(8,128)(2,1)}), bf16[64,32,128]{2,1,0:T(8,128)(2,1)}) %reduce-scatter.3.cloned.1.call-update) | async-done | bytes 524304 | tf_op jit(solution)/shard_map/reduce_scatter | solution.py:61
  177.1 1.5 bitcast_reduce_fusion
  178.6 2.2 fusion.28
  180.8 2.2 fusion.29
  183.1 1.3 add_convert_fusion.1
  184.4 1.1 copy.27
  185.8 53.3 %all-gather.5.cloned.1.call-done = bf16[32,512,128]{2,0,1:T(8,128)(2,1)} async-done(((bf16[32,64,128]{2,0,1:T(8,128)(2,1)}), bf16[32,512,128]{2,0,1:T(8,128)(2,1)}) %all-gather.5.cloned.1.call-update) | async-done | bytes 4194320 | tf_op jit(solution)/shard_map/all_gather | solution.py:79
  239.2 8.6 copy.29
  247.7 7.8 fusion.64
  255.5 13.6 %copy.33 = bf16[128,64,512]{0,1,2:T(8,128)(2,1)} copy(bf16[128,64,512]{2,1,0:T(8,128)(2,1)} %fusion.64) | data formatting | bytes 16777216 | tf_op jit(solution)/shard_map/ijc,ikc->jkc/dot_general | solution.py:84
  269.2 1.0 copy-done.17
  270.2 0.3 copy-done.20
  270.5 1.9 multiply_convert_fusion
  272.4 9.6 fusion.65
  281.9 2.4 copy.30
  284.3 56.9 %reduce-scatter.5.cloned.1.call-done = bf16[32,64,128]{2,1,0:T(8,128)(2,1)} async-done(((bf16[512,64,128]{2,1,0:T(8,128)(2,1)}), bf16[32,64,128]{2,1,0:T(8,128)(2,1)}) %reduce-scatter.5.cloned.1.call-update) | async-done | bytes 524304 | tf_op jit(solution)/shard_map/reduce_scatter | solution.py:83
  341.2 3.5 multiply_convert_fusion.1
  344.7 0.9 fusion.18
  345.7 0.3 fusion.44
  346.0 0.9 fusion.17
  346.9 0.9 fusion.16
  347.8 0.9 fusion.15
  348.8 0.9 fusion.14
  349.7 0.9 fusion.13
  350.6 0.8 broadcast_multiply_fusion
  351.4 1.4 convolution_add_fusion.3
  352.8 0.3 convolution_add_fusion.2
  353.1 0.3 convolution_add_fusion.1
  353.5 0.8 fusion.21
  354.3 1.3 fusion.30
  355.6 1.9 add_convert_fusion
  357.5 971.7 %all-reduce.2.cloned.1.call-done = f32[6,128,128]{2,1,0:T(8,128)} async-done(((f32[6,128,128]{2,1,0:T(8,128)}), f32[6,128,128]{2,1,0:T(8,128)}) %all-reduce.2.cloned.1.call-update) | async-done | bytes 393232 | tf_op jit(solution)/shard_map/psum | solution.py:120
  1329.2 1.8 copy.55
  (61 shorter events, 1.2 us)
Async XLA Ops:
  7.2 9.4 copy-start
  7.2 6.1 copy-start.1
  7.2 6.1 copy-start.11
  7.2 7.0 copy-start.14
  7.2 70.4 %all-gather.3.cloned.1.call-start = ((), (), s32[]{:S(2)}) async-start(), calls=%async_computation.2 | async-start | bytes 8912896 | tf_op jit(solution)/shard_map/all_gather | solution.py:59
  13.3 5.3 copy-start.4
  14.3 4.3 copy-start.2
  15.7 0.9 copy-start.5
  18.6 158.5 %reduce-scatter.3.cloned.1.call-start = ((), (), s32[]{:S(2)}) async-start(), calls=%async_computation.3 | async-start | bytes 4718592 | tf_op jit(solution)/shard_map/reduce_scatter | solution.py:61
  121.0 0.7 copy-start.15
  121.0 0.9 copy-start.12
  121.0 1.1 copy-start.16
  121.0 57.6 %copy-start.18 = (bf16[128,128]{1,0:T(8,128)(2,1)S(1)}, bf16[128,128]{1,0:T(8,128)(2,1)}, u32[]{:S(2)}) copy-start(bf16[128,128]{1,0:T(8,128)(2,1)} %param.18) | copy-start | bytes 98308
  121.0 118.1 %all-gather.5.cloned.1.call-start = ((), (), s32[]{:S(2)}) async-start(), calls=%async_computation.4 | async-start | bytes 4718592 | tf_op jit(solution)/shard_map/all_gather | solution.py:79
  177.1 6.0 copy-start.3
  185.6 155.6 %reduce-scatter.5.cloned.1.call-start = ((), (), s32[]{:S(2)}) async-start(), calls=%async_computation.5 | async-start | bytes 8912896 | tf_op jit(solution)/shard_map/reduce_scatter | solution.py:83
  269.1 1.0 copy-start.17
  269.1 1.4 copy-start.20
  269.2 1060.1 %all-reduce.2.cloned.1.call-start = ((), (), s32[]{:S(2)}) async-start(), calls=%async_computation.6 | async-start | bytes 786432 | tf_op jit(solution)/shard_map/psum | solution.py:120
  344.7 4.0 copy-start.6
  344.7 4.0 copy-start.8
  344.7 4.0 copy-start.9
  345.6 4.0 copy-start.19
  346.9 4.6 copy-start.13
  348.7 4.1 copy-start.7
  351.4 2.0 copy-start.10
Sparse Core Ops, SparseCore 0:
  18.7 58.8 all-gather.2
  121.1 55.9 reduce-scatter.2
  185.7 53.4 all-gather.4
  269.3 71.8 reduce-scatter.4
  351.5 977.6 all-reduce.1
where the time goes:
time: 1340 us
  waiting for transfers between devices  1190 us (89%)
  local copies, waits for them, and re-layouts  65.3 us (5%)
  matrix products  48.6 us (4%)
  other arithmetic  16.5 us (1%)
  between operations  14.2 us (1%)
    psum x1, waiting for transfers between devices, shards(): weight_grads = lax.psum(local_grads, ('row', 'col'))  972 us
    all_gather x1, waiting for transfers between devices, shards(): right_panel = lax.all_gather(right_edge, 'row', axis=0, tiled=True)  57.3 us
    reduce_scatter x1, waiting for transfers between devices, shards(): lax.psum_scatter(jnp.einsum('ijc,ikc->jkc', cotangent_panel, left_edge, p...  56.9 us
    all_gather x1, waiting for transfers between devices, shards(): cotangent_panel = lax.all_gather(grad_summed, 'col', axis=1, tiled=True)  53.3 us
    reduce_scatter x1, waiting for transfers between devices, shards(): lax.psum_scatter(jnp.einsum('jkc,ikc->jic', right_panel, left_edge, prefe...  53.2 us
  transfers between devices with their start and end apart: 5, of which 5 were waited for; matrix products, arithmetic and copies ran while one was open for 2% of the time, Pallas kernels for 0%

commit v1 on v0

--- a/solution.py
+++ b/solution.py
@@ -1,7 +1,102 @@
 import jax
 import jax.numpy as jnp
 from jax import lax
+from jax.experimental import pallas as pl
+from jax.experimental.pallas import tpu as pltpu
 from jax.sharding import PartitionSpec as P
+
+MESH = pl.DeviceIdType.MESH
+
+
+def for_peers(rows, cols, act):
+    row, col = lax.axis_index("row"), lax.axis_index("col")
+    order = sorted(range(cols), key=lambda step: min(step, cols - step))
+
+    def step(shift, carry):
+        for hop in order:
+
+            @pl.when(jnp.logical_or(shift > 0, hop > 0))
+            def _():
+                act(lax.rem(row + shift, rows), lax.rem(col + hop, cols))
+
+        return carry
+
+    lax.fori_loop(0, rows, step, 0)
+
+
+def wait_bytes(ref, sem):
+    pltpu.make_async_copy(ref, ref, sem).wait()
+
+
+def sum_kernel(rows, cols, parts_ref, out_ref, held, total, sems):
+    me = lax.axis_index("row") * cols + lax.axis_index("col")
+    others = rows * cols - 1
+    barrier = pltpu.get_barrier_semaphore()
+
+    def greet(row, col):
+        pl.semaphore_signal(
+            barrier, inc=1, device_id={"row": row, "col": col}, device_id_type=MESH
+        )
+
+    for_peers(rows, cols, greet)
+    pl.semaphore_wait(barrier, others)
+
+    def scatter(row, col):
+        pltpu.make_async_remote_copy(
+            src_ref=parts_ref.at[row * cols + col],
+            dst_ref=held.at[me],
+            send_sem=sems.at[0],
+            recv_sem=sems.at[1],
+            device_id={"row": row, "col": col},
+            device_id_type=MESH,
+        ).start()
+
+    for_peers(rows, cols, scatter)
+    held[me] = parts_ref[me]
+    wait_bytes(held.at[pl.ds(0, others)], sems.at[1])
+    total[...] = jnp.sum(held[...], axis=0)
+    out_ref[me] = total[...]
+
+    def spread(row, col):
+        pltpu.make_async_remote_copy(
+            src_ref=total,
+            dst_ref=out_ref.at[me],
+            send_sem=sems.at[2],
+            recv_sem=sems.at[3],
+            device_id={"row": row, "col": col},
+            device_id_type=MESH,
+        ).start()
+
+    for_peers(rows, cols, spread)
+    wait_bytes(held.at[pl.ds(0, others)], sems.at[0])
+    wait_bytes(held.at[pl.ds(0, others)], sems.at[2])
+    wait_bytes(held.at[pl.ds(0, others)], sems.at[3])
+
+
+def sum_over_part(values):
+    rows, cols = lax.axis_size("row"), lax.axis_size("col")
+    count, height, width = values.shape
+    devices = rows * cols
+    share = height // devices
+    parts = values.reshape(count, devices, share, width).transpose(1, 0, 2, 3)
+    parts = parts.reshape(devices, count * share, width)
+    out = pl.pallas_call(
+        lambda *refs: sum_kernel(rows, cols, *refs),
+        out_shape=jax.ShapeDtypeStruct(parts.shape, jnp.float32),
+        in_specs=[pl.BlockSpec(memory_space=pltpu.VMEM)],
+        out_specs=pl.BlockSpec(memory_space=pltpu.VMEM),
+        scratch_shapes=[
+            pltpu.VMEM(parts.shape, jnp.float32),
+            pltpu.VMEM(parts.shape[1:], jnp.float32),
+            pltpu.SemaphoreType.DMA((4,)),
+        ],
+        compiler_params=pltpu.CompilerParams(
+            collective_id=1, has_side_effects=True, vmem_limit_bytes=32 * 2**20
+        ),
+        name="weight_sum",
+    )(parts)
+    out = out.reshape(devices, count, share, width).transpose(1, 0, 2, 3)
+    return out.reshape(values.shape)
 
 
 def layer_norm(values):
@@ -117,7 +212,7 @@
             outer_sum(normed_sum, grad_projected),
         ]
     ) / jnp.float32(total)
-    weight_grads = lax.psum(local_grads, ("row", "col"))
+    weight_grads = sum_over_part(local_grads)
     return (result, grad_pair, weight_grads)
 
 

time: 1340 us -> 405 us (0.30)
  waiting for transfers between devices: 1190 us -> 220 us
  Pallas kernels: 0 us -> 38.3 us
    psum x1 -> x0, waiting for transfers between devices: 972 us -> none  [shards(): weight_grads = lax.psum(local_grads, ('row', 'col'))]
    pallas_call x0 -> x1, Pallas kernels: none -> 38.3 us  [sum_over_part(): pl.pallas_call(lambda *refs: sum_kernel(rows, cols, *refs), out_shape=jax...]
  transfers between devices with their start and end apart: 5 -> 4, of which waited for: 5 -> 4; matrix products, arithmetic and copies ran while one was open for 2% -> 5% of each run, Pallas kernels for 0% -> 0%
where the time goes in v1:
time: 405 us; the launch traced here: 403 us
  waiting for transfers between devices  220 us (54%)
  local copies, waits for them, and re-layouts  65.4 us (16%)
  matrix products  49.3 us (12%)
  Pallas kernels  38.3 us (9%)
  other arithmetic  15.8 us (4%)
  between operations  14.2 us (4%)
    all_gather x1, waiting for transfers between devices, shards(): right_panel = lax.all_gather(right_edge, 'row', axis=0, tiled=True)  57.3 us
    reduce_scatter x1, waiting for transfers between devices, shards(): lax.psum_scatter(jnp.einsum('ijc,ikc->jkc', cotangent_panel, left_edge, p...  55.9 us
    all_gather x1, waiting for transfers between devices, shards(): cotangent_panel = lax.all_gather(grad_summed, 'col', axis=1, tiled=True)  53.3 us
    reduce_scatter x1, waiting for transfers between devices, shards(): lax.psum_scatter(jnp.einsum('jkc,ikc->jic', right_panel, left_edge, prefe...  53.2 us
    pallas_call x1, Pallas kernels, sum_over_part(): pl.pallas_call(lambda *refs: sum_kernel(rows, cols, *refs), out_shape=jax...  38.3 us
    all_gather x1, local copies, waits for them, and re-layouts, shards(): right_panel = lax.all_gather(right_edge, 'row', axis=0, tiled=True)  23.7 us
    dot_general x1, local copies, waits for them, and re-layouts, shards(): jnp.einsum('ijc,ikc->jkc', cotangent_panel, left_edge, preferred_element_...  13.6 us
    dot_general x6, matrix products, project(): jnp.einsum('ijc,cd->ijd', source, weight, preferred_element_type=jnp.floa...  11.4 us
  transfers between devices with their start and end apart: 4, of which 4 were waited for; matrix products, arithmetic and copies ran while one was open for 5% of the time, Pallas kernels for 0%

profile of v1, /device:TPU:1, one launch (start us, length us, event | category | flops | bytes accessed | tf_op | source)
XLA Modules:
  0.0 403.2 jit_solution(13740816295833403752)
XLA Ops:
  7.3 0.7 convert_element_type.70
  8.1 1.4 convert_reduce_fusion
  9.5 1.7 fusion.13
  11.3 1.9 fusion.6
  13.3 0.9 fusion.41
  14.3 1.4 fusion.8
  15.7 0.9 copy-done.6
  16.6 2.0 multiply_convert_fusion.7
  18.7 1.6 copy.24
  20.3 57.3 %all-gather.3.cloned.1.call-done = bf16[512,64,128]{2,1,0:T(8,128)(2,1)} async-done(((bf16[32,64,128]{2,1,0:T(8,128)(2,1)}), bf16[512,64,128]{2,1,0:T(8,128)(2,1)}) %all-gather.3.cloned.1.call-update) | async-done | bytes 8388624 | tf_op jit(solution)/shard_map/all_gather | solution.py:154
  77.6 23.7 %copy.25 = bf16[512,64,128]{1,0,2:T(8,128)(2,1)} copy(bf16[512,64,128]{2,1,0:T(8,128)(2,1)} %all-gather.3.cloned.1.call-done) | data formatting | bytes 16777216 | tf_op jit(solution)/shard_map/all_gather | solution.py:154
  101.4 10.5 %convert_bitcast_fusion.1 = bf16[512,32,128]{0,1,2:T(8,128)(2,1)} fusion(bf16[32,64,128]{1,0,2:T(8,128)(2,1)S(1)} %copy.24, bf16[512,64,128]{1,0,2:T(8,128)(2,1)} %copy.25), kind=kOutput, calls=%fused_computation.1 | convolution fusion | flops 270532608 | bytes 13107200 | tf_op jit(solution)/shard_map/jkc,ikc->jic/dot_general | solution.py:157
  111.9 9.1 %copy.26 = bf16[512,32,128]{2,1,0:T(8,128)(2,1)} copy(bf16[512,32,128]{0,1,2:T(8,128)(2,1)} %convert_bitcast_fusion.1) | data formatting | bytes 8388608 | tf_op jit(solution)/shard_map/convert_element_type | solution.py:159
  121.1 0.6 copy-done.16
  122.1 1.9 multiply_convert_fusion.5
  123.9 53.2 %reduce-scatter.3.cloned.1.call-done = bf16[64,32,128]{2,1,0:T(8,128)(2,1)} async-done(((bf16[512,32,128]{2,1,0:T(8,128)(2,1)}), bf16[64,32,128]{2,1,0:T(8,128)(2,1)}) %reduce-scatter.3.cloned.1.call-update) | async-done | bytes 524304 | tf_op jit(solution)/shard_map/reduce_scatter | solution.py:156
  177.1 1.5 bitcast_reduce_fusion
  178.6 2.2 fusion.22
  180.8 2.2 fusion.23
  183.1 1.3 add_convert_fusion.1
  184.4 1.1 copy.28
  185.6 0.2 reduce-scatter.5.cloned.1.call-start
  185.8 53.3 %all-gather.5.cloned.1.call-done = bf16[32,512,128]{2,0,1:T(8,128)(2,1)} async-done(((bf16[32,64,128]{2,0,1:T(8,128)(2,1)}), bf16[32,512,128]{2,0,1:T(8,128)(2,1)}) %all-gather.5.cloned.1.call-update) | async-done | bytes 4194320 | tf_op jit(solution)/shard_map/all_gather | solution.py:174
  239.2 8.6 %copy.30 = bf16[32,512,128]{1,0,2:T(8,128)(2,1)} copy(bf16[32,512,128]{2,0,1:T(8,128)(2,1)} %all-gather.5.cloned.1.call-done) | data formatting | bytes 8388608 | tf_op jit(solution)/shard_map/all_gather | solution.py:174
  247.7 7.8 %fusion.64 = bf16[128,64,512]{2,1,0:T(8,128)(2,1)} fusion(bf16[32,64,128]{1,0,2:T(8,128)(2,1)S(1)} %copy.24, bf16[32,512,128]{1,0,2:T(8,128)(2,1)} %copy.30), kind=kOutput, calls=%fused_computation.92 | convolution fusion | flops 268435456 | bytes 13107200 | tf_op jit(solution)/shard_map/ijc,ikc->jkc/dot_general | solution.py:179
  255.5 13.6 %copy.34 = bf16[128,64,512]{0,1,2:T(8,128)(2,1)} copy(bf16[128,64,512]{2,1,0:T(8,128)(2,1)} %fusion.64) | data formatting | bytes 16777216 | tf_op jit(solution)/shard_map/ijc,ikc->jkc/dot_general | solution.py:179
  269.2 1.0 copy-done.18
  270.2 3.3 multiply_convert_fusion
  273.5 0.9 fusion.49
  274.4 0.9 fusion.25
  275.4 7.6 %fusion.65 = f32[128,64,32]{1,2,0:T(8,128)S(1)} fusion(bf16[32,512,128]{1,0,2:T(8,128)(2,1)S(1)} %copy-done.1, bf16[512,64,128]{1,0,2:T(8,128)(2,1)} %copy.25), kind=kOutput, calls=%fused_computation.93 | convolution fusion | flops 268435456 | bytes 13631488 | tf_op jit(solution)/shard_map/ijc,jkc->ikc/dot_general | solution.py:175
  283.0 2.4 copy.31
  285.3 55.9 %reduce-scatter.5.cloned.1.call-done = bf16[32,64,128]{2,1,0:T(8,128)(2,1)} async-done(((bf16[512,64,128]{2,1,0:T(8,128)(2,1)}), bf16[32,64,128]{2,1,0:T(8,128)(2,1)}) %reduce-scatter.5.cloned.1.call-update) | async-done | bytes 524304 | tf_op jit(solution)/shard_map/reduce_scatter | solution.py:178
  341.2 3.5 multiply_convert_fusion.1
  344.7 0.9 fusion.57
  345.6 0.3 fusion.39
  345.9 0.9 fusion.51
  346.8 1.5 fusion.53
  348.4 1.6 fusion.55
  349.9 1.4 stack.27
  351.4 38.3 %weight_sum.1 = f32[128,6,128]{2,1,0:T(8,128)S(1)} custom-call(f32[128,6,128]{2,1,0:T(8,128)S(1)} %multiply_bitcast_fusion.refs_0_), custom_call_target="tpu_custom_call" | custom-call | tf_op jit(solution)/shard_map/weight_sum/pallas_call | solution.py:83
  389.7 0.8 copy.35
  390.5 1.4 convolution_add_fusion.3
  391.9 0.3 convolution_add_fusion.2
  392.3 0.3 convolution_add_fusion.1
  392.6 0.8 fusion.15
  393.4 1.3 fusion.24
  394.7 1.9 add_convert_fusion
  (60 shorter events, 1.0 us)
Async XLA Ops:
  7.2 9.4 %copy-start = (bf16[128,128]{1,0:T(8,128)(2,1)S(1)}, bf16[128,128]{1,0:T(8,128)(2,1)}, u32[]{:S(2)}) copy-start(bf16[128,128]{1,0:T(8,128)(2,1)} %param.15) | copy-start | bytes 98308
  7.2 6.1 %copy-start.2 = (bf16[32,64,128]{2,1,0:T(8,128)(2,1)S(1)}, bf16[32,64,128]{2,1,0:T(8,128)(2,1)}, u32[]{:S(2)}) copy-start(bf16[32,64,128]{2,1,0:T(8,128)(2,1)} %param.10) | copy-start | bytes 1572868
  7.2 6.1 %copy-start.10 = (bf16[128,128]{1,0:T(8,128)(2,1)S(1)}, bf16[128,128]{1,0:T(8,128)(2,1)}, u32[]{:S(2)}) copy-start(bf16[128,128]{1,0:T(8,128)(2,1)} %param.13) | copy-start | bytes 98308
  7.2 7.0 %copy-start.14 = (bf16[128,128]{1,0:T(8,128)(2,1)S(1)}, bf16[128,128]{1,0:T(8,128)(2,1)}, u32[]{:S(2)}) copy-start(bf16[128,128]{1,0:T(8,128)(2,1)} %param.16) | copy-start | bytes 98308
  7.2 70.4 %all-gather.3.cloned.1.call-start = ((), (), s32[]{:S(2)}) async-start(), calls=%async_computation.2 | async-start | bytes 8912896 | tf_op jit(solution)/shard_map/all_gather | solution.py:154
  13.3 5.3 %copy-start.5 = (f32[32,64,128]{2,1,0:T(8,128)}, f32[32,64,128]{2,1,0:T(8,128)S(1)}, u32[]{:S(2)}) copy-start(f32[32,64,128]{2,1,0:T(8,128)S(1)} %fusion.6) | copy-start | bytes 3145732
  14.3 4.3 %copy-start.3 = (f32[32,64,128]{2,1,0:T(8,128)}, f32[32,64,128]{2,1,0:T(8,128)S(1)}, u32[]{:S(2)}) copy-start(f32[32,64,128]{2,1,0:T(8,128)S(1)} %fusion.41) | copy-start | bytes 3145732
  15.7 0.9 copy-start.6
  18.6 158.5 %reduce-scatter.3.cloned.1.call-start = ((), (), s32[]{:S(2)}) async-start(), calls=%async_computation.3 | async-start | bytes 4718592 | tf_op jit(solution)/shard_map/reduce_scatter | solution.py:156
  121.0 0.7 copy-start.16
  121.0 0.9 copy-start.11
  121.0 1.1 copy-start.17
  121.0 57.6 %copy-start.19 = (bf16[128,128]{1,0:T(8,128)(2,1)S(1)}, bf16[128,128]{1,0:T(8,128)(2,1)}, u32[]{:S(2)}) copy-start(bf16[128,128]{1,0:T(8,128)(2,1)} %param.18) | copy-start | bytes 98308
  121.0 118.1 %all-gather.5.cloned.1.call-start = ((), (), s32[]{:S(2)}) async-start(), calls=%async_computation.4 | async-start | bytes 4718592 | tf_op jit(solution)/shard_map/all_gather | solution.py:174
  177.1 6.0 %copy-start.4 = (bf16[64,32,128]{2,1,0:T(8,128)(2,1)S(1)}, bf16[64,32,128]{2,1,0:T(8,128)(2,1)}, u32[]{:S(2)}) copy-start(bf16[64,32,128]{2,1,0:T(8,128)(2,1)} %reduce-scatter.3.cloned.1.call-done) | copy-start | bytes 1572868
  185.6 155.6 %reduce-scatter.5.cloned.1.call-start = ((), (), s32[]{:S(2)}) async-start(), calls=%async_computation.5 | async-start | bytes 8912896 | tf_op jit(solution)/shard_map/reduce_scatter | solution.py:178
  269.1 1.0 copy-start.18
  269.2 5.3 %copy-start.20 = (bf16[32,64,128]{2,1,0:T(8,128)(2,1)S(1)}, bf16[32,64,128]{2,1,0:T(8,128)(2,1)}, u32[]{:S(2)}) copy-start(bf16[32,64,128]{2,1,0:T(8,128)(2,1)} %get-tuple-element.23) | copy-start | bytes 1572868
  269.2 6.2 %copy-start.1 = (bf16[32,512,128]{1,0,2:T(8,128)(2,1)S(1)}, bf16[32,512,128]{1,0,2:T(8,128)(2,1)}, u32[]{:S(2)}) copy-start(bf16[32,512,128]{1,0,2:T(8,128)(2,1)} %copy.30) | copy-start | bytes 12582916
  273.5 0.9 copy-start.8
  344.7 5.2 %copy-start.7 = (bf16[32,64,128]{2,1,0:T(8,128)(2,1)}, bf16[32,64,128]{2,1,0:T(8,128)(2,1)S(1)}, u32[]{:S(2)}) copy-start(bf16[32,64,128]{2,1,0:T(8,128)(2,1)S(1)} %get-tuple-element.18) | copy-start | bytes 1572868
  345.9 44.6 %copy-start.13 = (bf16[128,128]{1,0:T(8,128)(2,1)S(1)}, bf16[128,128]{1,0:T(8,128)(2,1)}, u32[]{:S(2)}) copy-start(bf16[128,128]{1,0:T(8,128)(2,1)} %param.14) | copy-start | bytes 98308
  351.3 40.9 %copy-start.15 = (bf16[128,128]{1,0:T(8,128)(2,1)S(1)}, bf16[128,128]{1,0:T(8,128)(2,1)}, u32[]{:S(2)}) copy-start(bf16[128,128]{1,0:T(8,128)(2,1)} %param.16) | copy-start | bytes 98308
  390.5 2.0 copy-start.9
  390.5 2.0 copy-start.12
Sparse Core Ops, SparseCore 0:
  18.7 58.8 all-gather.2
  121.2 55.9 reduce-scatter.2
  185.7 53.3 all-gather.4
  269.3 71.8 reduce-scatter.4

commit v2 on v0

v2 whole, which is shorter than its diff:
```python
import functools

import jax
import jax.numpy as jnp
from jax import lax
from jax.experimental import pallas as pl
from jax.experimental.pallas import tpu as pltpu
from jax.sharding import PartitionSpec as P

MESH = pl.DeviceIdType.MESH
F32 = jnp.float32
BF16 = jnp.bfloat16
EPS = 1e-05


def dot_nn(left, right):
    return jnp.dot(left, right, preferred_element_type=F32)


def dot_nt(left, right):
    return lax.dot_general(left, right, (((1,), (1,)), ((), ())), preferred_element_type=F32)


def dot_tn(left, right):
    return lax.dot_general(left, right, (((0,), (0,)), ((), ())), preferred_element_type=F32)


def mean_rows(values):
    return jnp.mean(values, axis=0, keepdims=True)


def wait_bytes(ref, sem):
    pltpu.make_async_copy(ref, ref, sem).wait()


def kernel(
    rows,
    cols,
    pair,
    cot,
    pad_row,
    crop_row,
    pad_col,
    crop_col,
    left_proj,
    left_gate,
    right_proj,
    right_gate,
    out_gate,
    out_proj,
    result,
    grad_pair,
    weight_grads,
    send_l,
    send_r,
    send_s,
    send_g,
    send_dl,
    send_dr,
    recv_l,
    recv_r,
    recv_s,
    recv_g,
    recv_dl,
    recv_dr,
    stage,
    spread,
    norm_t,
    xhat,
    scale,
    left_v,
    left_s,
    right_v,
    right_s,
    gate_c,
    gate_u,
    grad_ns,
    grad_n,
    norm_s,
    grad_p,
    grad_o,
    grad_e,
    w_left,
    w_right,
    w_out,
    w_proj,
    b_left,
    b_right,
    part_a,
    held_a,
    line_a,
    full_a,
    part_b,
    held_b,
    line_b,
    full_b,
    sems,
):
    row, col = lax.axis_index("row"), lax.axis_index("col")
    me = row * cols + col
    channels = rows * cols
    tiles, half_lanes = pair.shape[0] // 2, pair.shape[1]
    order = sorted(range(cols), key=lambda step: min(step, cols - step))
    barrier = pltpu.get_barrier_semaphore()

    def device(r, c):
        return {"row": r, "col": c}

    def for_rows(act, itself):
        def step(shift, carry):
            act(lax.rem(row + shift, rows))
            return carry

        lax.fori_loop(0 if itself else 1, rows, step, 0)

    def for_peers(act):
        def step(shift, carry):
            for hop in order[1:]:
                act(lax.rem(row + shift, rows), lax.rem(col + hop, cols))

            @pl.when(shift > 0)
            def _():
                act(lax.rem(row + shift, rows), col)

            return carry

        lax.fori_loop(0, rows, step, 0)

    def copy_to(src, dst, which, r, c):
        pltpu.make_async_remote_copy(
            src_ref=src,
            dst_ref=dst,
            send_sem=sems.at[2 * which],
            recv_sem=sems.at[2 * which + 1],
            device_id=device(r, c),
            device_id_type=MESH,
        ).start()

    def at_owner(ref, r, c):
        return ref.at[c, pl.ds(pl.multiple_of(r * tiles, tiles), tiles)]

    def to_owners(src, dst, which):
        dst[col, pl.ds(pl.multiple_of(row * tiles, tiles), tiles)] = src[me]
        for_peers(
            lambda r, c: copy_to(src.at[r * cols + c], at_owner(dst, row, col), which, r, c)
        )

    def from_owner(src, dst, which, r, c):
        copy_to(at_owner(src, r, c), dst.at[me], which, r, c)

    def arrived(which):
        wait_bytes(send_l.at[pl.ds(0, channels - 1)], sems.at[2 * which + 1])

    def sent(which):
        wait_bytes(send_l.at[pl.ds(0, channels - 1)], sems.at[2 * which])

    def for_tiles(body, unroll=2):
        def step(p, carry):
            body(p)
            return carry

        lax.fori_loop(0, tiles, step, 0, unroll=unroll)

    def lanes(p):
        return pl.ds(pl.multiple_of(p * 2 * half_lanes, 2 * half_lanes), 2 * half_lanes)

    def strided(p):
        return pl.ds(p, channels, stride=tiles)

    def pack(dst):
        dst[...] = stage[...].reshape(channels, tiles, 2 * half_lanes).astype(BF16)

    def unpack(src):
        stage[...] = src[...].astype(F32).reshape(channels * tiles, 2 * half_lanes)

    low = lax.broadcasted_iota(jnp.int32, (1, 2 * half_lanes), 1) < half_lanes

    def mask_of(row_ref, col_ref):
        line = col_ref[pl.ds(col, 1), :].astype(F32)
        line = jnp.concatenate([line, line], axis=1)

        def mask(p):
            first = row_ref[row * 2 * tiles + p].astype(F32)
            second = row_ref[row * 2 * tiles + tiles + p].astype(F32)
            return jnp.where(low, first, second) * line

        return mask

    pad, crop = mask_of(pad_row, pad_col), mask_of(crop_row, crop_col)

    def tile_t(ref, p):
        both = jnp.concatenate([ref[p], ref[p + tiles]], axis=0)
        return both.astype(F32).T

    def put_tile(ref, p, values):
        back = values.T.astype(BF16)
        ref[p] = back[:half_lanes]
        ref[p + tiles] = back[half_lanes:]

    for_peers(
        lambda r, c: pl.semaphore_signal(
            barrier, inc=1, device_id=device(r, c), device_id_type=MESH
        )
    )

    def flip(ref):
        return ref[...].astype(F32).T.astype(BF16)

    size = left_proj.shape[0]
    w_left[:size] = flip(left_proj)
    w_left[size:] = flip(left_gate)
    w_right[:size] = flip(right_proj)
    w_right[size:] = flip(right_gate)
    w_out[...] = flip(out_gate)
    w_proj[...] = flip(out_proj)
    b_left[:, :size] = left_proj[...]
    b_left[:, size:] = left_gate[...]
    b_right[:, :size] = right_proj[...]
    b_right[:, size:] = right_gate[...]

    def edge(p, normed, weight, value_ref, sig_ref):
        both = dot_nn(weight[...], normed)
        value, sig = both[:size], jax.nn.sigmoid(both[size:])
        value_ref[p] = value
        sig_ref[p] = sig
        stage[strided(p), :] = pad(p) * sig * value

    def left_tile(p):
        wide = tile_t(pair, p)
        center = wide - mean_rows(wide)
        rstd = lax.rsqrt(mean_rows(center * center) + EPS)
        hat = center * rstd
        xhat[p] = hat
        scale[p] = rstd
        normed = hat.astype(BF16)
        norm_t[:, lanes(p)] = normed
        edge(p, normed, w_left, left_v, left_s)

    for_tiles(left_tile)
    pack(send_l)
    pl.semaphore_wait(barrier, channels - 1)
    to_owners(send_l, recv_l, 0)
    for_tiles(lambda p: edge(p, norm_t[:, lanes(p)], w_right, right_v, right_s))
    pack(send_r)
    to_owners(send_r, recv_r, 1)

    def out_tile(p):
        gate = jax.nn.sigmoid(dot_nn(w_out[...], norm_t[:, lanes(p)]))
        upstream = crop(p) * tile_t(cot, p)
        projected_grad = (upstream * gate).astype(BF16)
        grad_p[:, lanes(p)] = projected_grad
        gate_c[p] = crop(p) * gate
        gate_u[p] = upstream * gate * (1.0 - gate)
        grad_ns[p] = dot_nn(out_proj[...], projected_grad)

    for_tiles(out_tile)

    width = 2 * half_lanes
    arrived(0)
    arrived(1)

    def spread_block(c, carry):
        raw = recv_r[c].astype(F32)
        turned = pltpu.roll(raw, half_lanes, 1)
        raw = raw.reshape(cols, rows // cols, tiles, width)
        turned = turned.reshape(cols, rows // cols, tiles, width)
        zero = jnp.zeros_like(raw)
        top = jnp.stack([jnp.where(low, raw, zero), jnp.where(low, turned, zero)], axis=2)
        bottom = jnp.stack([jnp.where(low, zero, turned), jnp.where(low, zero, raw)], axis=2)
        both = jnp.stack([top, bottom], axis=1)
        spread[:, lanes(c)] = both.reshape(cols * width, width).astype(BF16)
        return carry

    lax.fori_loop(0, cols, spread_block, 0)

    def whole(ref):
        return jnp.concatenate([ref[c] for c in range(cols)], axis=1)

    def send_column(src, dst, which, c, hop):
        for_rows(lambda r: from_owner(src, dst, which, r, c), hop != 0)

    def keep_own(src, dst):
        dst[me] = src[col, pl.ds(pl.multiple_of(row * tiles, tiles), tiles)]

    for hop in order[1:] + order[:1]:
        c = lax.rem(col + hop, cols)
        send_s[c] = dot_nt(whole(recv_l), spread[lanes(c), :]).astype(BF16)
        send_column(send_s, recv_s, 2, c, hop)
    keep_own(send_s, recv_s)

    arrived(2)
    unpack(recv_s)

    def sum_tile(p):
        sums = stage[strided(p), :]
        center = sums - mean_rows(sums)
        rstd = lax.rsqrt(mean_rows(center * center) + EPS)
        hat = center * rstd
        norm_s[:, lanes(p)] = hat.astype(BF16)
        grad = grad_ns[p]
        grad = rstd * (grad - mean_rows(grad) - hat * mean_rows(grad * hat))
        stage[strided(p), :] = grad

    for_tiles(sum_tile)
    pack(send_g)
    to_owners(send_g, recv_g, 3)

    def result_tile(p):
        projected = dot_nn(w_proj[...], norm_s[:, lanes(p)])
        put_tile(result, p, gate_c[p] * projected)
        logit = (gate_u[p] * projected).astype(BF16)
        grad_o[:, lanes(p)] = logit
        grad_n[p] = dot_nn(out_gate[...], logit)

    for_tiles(result_tile)
    inverse = 1.0 / (rows * 2 * tiles)

    def put_weight(ref, place, values):
        high = size // rows
        ref[:, place * high : (place + 1) * high, :] = (values * inverse).reshape(
            rows, high, size
        )

    put_weight(part_a, 2, dot_nt(norm_t[...], grad_o[...]))
    put_weight(part_a, 3, dot_nt(norm_s[...], grad_p[...]))

    arrived(3)
    for hop in order[1:] + order[:1]:
        c = lax.rem(col + hop, cols)
        send_dl[c] = dot_nn(whole(recv_g), spread[:, lanes(c)]).astype(BF16)
        send_column(send_dl, recv_dl, 4, c, hop)
    keep_own(send_dl, recv_dl)

    per = rows // cols

    def right_block(c, carry):
        outer = dot_tn(recv_g[c], whole(recv_l))
        for k in range(cols):
            part = outer[:, k * width : (k + 1) * width].reshape(2, per, 2, tiles, width)
            keep = jnp.where(low, part[0, :, 0], part[1, :, 1])
            turn = jnp.where(low, part[0, :, 1], part[1, :, 0])
            turn = pltpu.roll(turn.reshape(per * tiles, width), half_lanes, 1)
            at = pl.ds(pl.multiple_of(c * per * tiles, per * tiles), per * tiles)
            send_dr[k, at, :] = (keep.reshape(per * tiles, width) + turn).astype(BF16)
        return carry

    lax.fori_loop(0, cols, right_block, 0)
    for_peers(lambda r, c: from_owner(send_dr, recv_dr, 5, r, c))
    keep_own(send_dr, recv_dr)

    def weight_parts(part, held, which):
        held[row] = part[row]
        for_rows(lambda r: copy_to(part.at[r], held.at[row], which, r, col), False)

    def weight_lines(held, line, which):
        wait_bytes(held.at[pl.ds(0, rows - 1)], sems.at[2 * which + 1])
        line[col] = jnp.sum(held[...], axis=0)
        for hop in order[1:]:
            copy_to(line.at[col], line.at[col], which + 1, row, lax.rem(col + hop, cols))

    def weight_full(line, full, which):
        wait_bytes(line.at[pl.ds(0, cols - 1)], sems.at[2 * which + 3])
        full[row] = jnp.sum(line[...], axis=0)
        for_rows(lambda r: copy_to(full.at[row], full.at[row], which + 2, r, col), False)

    def weight_done(line, full, which, places):
        wait_bytes(full.at[pl.ds(0, rows - 1)], sems.at[2 * which + 5])
        high = size // rows
        for slot, place in enumerate(places):
            part = full[:, slot * high : (slot + 1) * high, :]
            weight_grads[place] = part.reshape(size, size)
        wait_bytes(full.at[pl.ds(0, rows - 1)], sems.at[2 * which])
        wait_bytes(line.at[pl.ds(0, cols - 1)], sems.at[2 * which + 2])
        wait_bytes(full.at[pl.ds(0, rows - 1)], sems.at[2 * which + 4])

    def edge_grads(p, value_ref, sig_ref):
        grad, sig = pad(p) * stage[strided(p), :], sig_ref[p]
        grad_v = grad * sig
        grad_e[:size, lanes(p)] = grad_v.astype(BF16)
        grad_e[size:, lanes(p)] = (grad_v * value_ref[p] * (1.0 - sig)).astype(BF16)

    arrived(4)
    unpack(recv_dl)

    def left_back(p):
        edge_grads(p, left_v, left_s)
        grad_n[p] += dot_nn(b_left[...], grad_e[:, lanes(p)])

    for_tiles(left_back)
    both = dot_nt(norm_t[...], grad_e[...])
    put_weight(part_a, 0, both[:, :size])
    put_weight(part_a, 1, both[:, size:])
    weight_parts(part_a, held_a, 6)
    weight_lines(held_a, line_a, 6)
    weight_full(line_a, full_a, 6)

    arrived(5)
    unpack(recv_dr)
    for_tiles(lambda p: edge_grads(p, right_v, right_s))
    both = dot_nt(norm_t[...], grad_e[...])
    put_weight(part_b, 0, both[:, :size])
    put_weight(part_b, 1, both[:, size:])
    weight_parts(part_b, held_b, 9)

    def pair_tile(p):
        grad = grad_n[p] + dot_nn(b_right[...], grad_e[:, lanes(p)])
        hat = xhat[p]
        grad = scale[p] * (grad - mean_rows(grad) - hat * mean_rows(grad * hat))
        put_tile(grad_pair, p, grad)

    for_tiles(pair_tile)
    weight_lines(held_b, line_b, 9)
    weight_full(line_b, full_b, 9)
    weight_done(line_a, full_a, 6, (0, 1, 4, 5))
    weight_done(line_b, full_b, 9, (2, 3))
    for which in range(6):
        sent(which)


def shards(
    pair,
    pad_mask,
    crop_mask,
    left_proj,
    left_gate,
    right_proj,
    right_gate,
    out_gate,
    out_proj,
    cotangent,
):
    rows, cols = lax.axis_size("row"), lax.axis_size("col")
    high, wide, size = pair.shape
    tiles, width, channels = high // 2, 2 * wide, rows * cols
    positions = tiles * width
    vmem = pl.BlockSpec(memory_space=pltpu.VMEM)
    smem = pl.BlockSpec(memory_space=pltpu.SMEM)
    at_home = pltpu.VMEM((channels, tiles, width), BF16)
    at_owner = pltpu.VMEM((cols, rows * tiles, width), BF16)
    wide_tiles = pltpu.VMEM((tiles, size, width), F32)
    flat = pltpu.VMEM((size, positions), BF16)
    pair_weights = pltpu.VMEM((2 * size, size), BF16)
    weight = pltpu.VMEM((size, size), BF16)
    back_weights = pltpu.VMEM((size, 2 * size), BF16)
    share = size // rows

    def sum_buffers(count):
        return [
            pltpu.VMEM((rows, count * share, size), F32),
            pltpu.VMEM((rows, count * share, size), F32),
            pltpu.VMEM((cols, count * share, size), F32),
            pltpu.VMEM((rows, count * share, size), F32),
        ]

    return pl.pallas_call(
        functools.partial(kernel, rows, cols),
        out_shape=(
            jax.ShapeDtypeStruct(pair.shape, BF16),
            jax.ShapeDtypeStruct(pair.shape, BF16),
            jax.ShapeDtypeStruct((6, size, size), F32),
        ),
        in_specs=[vmem, vmem, smem, smem] + [vmem] * 8,
        out_specs=(vmem, vmem, vmem),
        scratch_shapes=[
            at_home,
            at_home,
            at_owner,
            at_home,
            at_owner,
            at_owner,
            at_owner,
            at_owner,
            at_home,
            at_owner,
            at_home,
            at_home,
            pltpu.VMEM((channels * tiles, width), F32),
            pltpu.VMEM((cols * width, cols * width), BF16),
            flat,
            wide_tiles,
            pltpu.VMEM((tiles, 1, width), F32),
            wide_tiles,
            wide_tiles,
            wide_tiles,
            wide_tiles,
            wide_tiles,
            wide_tiles,
            wide_tiles,
            wide_tiles,
            flat,
            flat,
            flat,
            pltpu.VMEM((2 * size, positions), BF16),
            pair_weights,
            pair_weights,
            weight,
            weight,
            back_weights,
            back_weights,
            *sum_buffers(4),
            *sum_buffers(2),
            pltpu.SemaphoreType.DMA((24,)),
        ],
        compiler_params=pltpu.CompilerParams(
            collective_id=1, has_side_effects=True, vmem_limit_bytes=50 * 2**20
        ),
        name="triangle",
    )(
        pair,
        cotangent,
        pad_mask,
        crop_mask,
        pad_mask.reshape(cols, wide),
        crop_mask.reshape(cols, wide),
        left_proj,
        left_gate,
        right_proj,
        right_gate,
        out_gate,
        out_proj,
    )


def solution(mesh):
    blocks = P(("rep", "row"), "col", None)
    return jax.shard_map(
        shards,
        mesh=mesh,
        in_specs=(blocks, P("rep"), P("rep"), P(), P(), P(), P(), P(), P(), blocks),
        out_specs=(blocks, blocks, P("rep", None, None)),
        check_vma=False,
    )
```

time: 1340 us -> 138 us (0.10)
  waiting for transfers between devices: 1190 us -> 0 us
  Pallas kernels: 0 us -> 127 us
  local copies, waits for them, and re-layouts: 65.3 us -> 10.4 us
  matrix products: 48.6 us -> 0 us
  other arithmetic: 16.5 us -> 0 us
  between operations: 14.2 us -> 0.66 us
    psum x1 -> x0, waiting for transfers between devices: 972 us -> none  [shards(): weight_grads = lax.psum(local_grads, ('row', 'col'))]
    pallas_call x0 -> x1, Pallas kernels: none -> 127 us  [shards(): pl.pallas_call(functools.partial(kernel, rows, cols), out_shape=(jax.Shap...]
    all_gather x2 -> x0, waiting for transfers between devices: 111 us -> none  [the longest x1 57.3 us: shards(): right_panel = lax.all_gather(right_edge, 'row', axis=0, tiled=True)]
    reduce_scatter x2 -> x0, waiting for transfers between devices: 110 us -> none  [the longest x1 56.9 us: shards(): lax.psum_scatter(jnp.einsum('ijc,ikc->jkc', cotangent_panel, left_edge, p...]
    dot_general x21 -> x0, matrix products: 48.6 us -> none  [the longest x1 10.5 us: shards(): jnp.einsum('jkc,ikc->jic', right_panel, left_edge, preferred_element_type...]
    all_gather x2 -> x0, local copies, waits for them, and re-layouts: 32.3 us -> none  [the longest x1 23.7 us: shards(): right_panel = lax.all_gather(right_edge, 'row', axis=0, tiled=True)]
    dot_general x2 -> x0, local copies, waits for them, and re-layouts: 16 us -> none  [the longest x1 13.6 us: shards(): jnp.einsum('ijc,ikc->jkc', cotangent_panel, left_edge, preferred_element_...]
  transfers between devices with their start and end apart: 5 -> 0, of which waited for: 5 -> 0; matrix products, arithmetic and copies ran while one was open for 2% -> 0% of each run, Pallas kernels for 0% -> 0%
where the time goes in v2:
time: 138 us
  Pallas kernels  127 us (92%)
  local copies, waits for them, and re-layouts  10.4 us (8%)
    pallas_call x1, Pallas kernels, shards(): pl.pallas_call(functools.partial(kernel, rows, cols), out_shape=(jax.Shap...  127 us
    unnamed x23, local copies, waits for them, and re-layouts  9.57 us

profile of v2, /device:TPU:1, one launch (start us, length us, event | category | flops | bytes accessed | tf_op | source)
XLA Modules:
  0.0 137.7 jit_solution(14592674513427464334)
XLA Ops:
  0.6 0.0 copy-start.9
  0.6 0.8 reshape.12.pad_col
  1.4 0.0 copy-done.9
  1.4 0.0 copy-start.8
  1.4 0.1 reshape.13.crop_col
  1.5 0.6 copy-done.8
  2.1 0.0 copy-start
  2.1 1.0 copy-done
  3.1 0.0 copy-start.1
  3.1 1.0 copy-done.1
  4.2 0.0 copy-start.2
  4.2 0.8 copy-done.2
  4.9 0.0 copy-start.3
  4.9 0.8 copy-done.3
  5.7 0.0 copy-start.4
  5.7 0.8 copy-done.4
  6.4 0.0 copy-start.5
  6.4 0.8 copy-done.5
  7.2 0.0 copy-start.6
  7.2 0.8 copy-done.6
  8.0 0.0 copy-start.7
  8.0 0.8 copy-done.7
  8.7 126.6 %triangle.1 = (bf16[32,64,128]{2,1,0:T(8,128)(2,1)S(1)}, bf16[32,64,128]{2,1,0:T(8,128)(2,1)S(1)}, f32[6,128,128]{2,1,0:T(8,128)S(1)}) custom-call(bf16[32,64,128]{2,1,0:T(8,128)(2,1)S(1)} %copy-done, bf16[32,64,128]{2,1,0:T(8,128)(2,1)S(1)} %copy-done.1, s32[512]{0:T(512)S(1)} %copy-done.8, s32[512]{0:T(512)S(1)} %copy-done.9, ...), custom_call_target="tpu_custom_call" | custom-call | tf_op jit(solution)/shard_map/triangle/pallas_call | solution.py:455
  135.4 0.8 copy.16
  136.1 0.8 copy.17
  136.9 0.7 copy.18
Async XLA Ops:
  0.6 0.8 copy-start.9
  1.4 0.7 copy-start.8
  2.1 1.0 copy-start
  3.1 1.0 copy-start.1
  4.2 0.8 copy-start.2
  4.9 0.8 copy-start.3
  5.7 0.8 copy-start.4
  6.4 0.8 copy-start.5
  7.2 0.8 copy-start.6
  8.0 0.8 copy-start.7

commit v3 on v2

v3 whole, which is shorter than its diff:
```python
import functools

import jax
import jax.numpy as jnp
from jax import lax
from jax.experimental import pallas as pl
from jax.experimental.pallas import tpu as pltpu
from jax.sharding import PartitionSpec as P

MESH = pl.DeviceIdType.MESH
F32 = jnp.float32
BF16 = jnp.bfloat16
EPS = 1e-05
PARTS = 2
LEFT, RIGHT, SUMS, GRADS, LEFT_GRADS, RIGHT_GRADS = (PARTS * n for n in range(6))
WEIGHTS_A, WEIGHTS_B = 6 * PARTS, 6 * PARTS + 3


def dot_nn(left, right):
    return jnp.dot(left, right, preferred_element_type=F32)


def dot_nt(left, right):
    return lax.dot_general(left, right, (((1,), (1,)), ((), ())), preferred_element_type=F32)


def dot_tn(left, right):
    return lax.dot_general(left, right, (((0,), (0,)), ((), ())), preferred_element_type=F32)


def mean_rows(values):
    return jnp.mean(values, axis=0, keepdims=True)


def wait_bytes(ref, sem):
    pltpu.make_async_copy(ref, ref, sem).wait()


def kernel(
    rows,
    cols,
    pair_in,
    cot_in,
    pad_in,
    crop_in,
    left_proj_in,
    left_gate_in,
    right_proj_in,
    right_gate_in,
    out_gate_in,
    out_proj_in,
    result,
    grad_pair,
    weight_grads,
    pair,
    cot,
    pad_mask,
    crop_mask,
    left_proj,
    left_gate,
    right_proj,
    right_gate,
    out_gate,
    out_proj,
    in_sems,
    send_l,
    send_r,
    send_s,
    send_g,
    send_dl,
    send_dr,
    recv_l,
    recv_r,
    recv_s,
    recv_g,
    recv_dl,
    recv_dr,
    stage,
    spread,
    mat_l,
    mat_g,
    norm_t,
    xhat,
    scale,
    left_v,
    left_s,
    right_v,
    right_s,
    gate_c,
    gate_u,
    grad_ns,
    grad_n,
    norm_s,
    grad_p,
    grad_o,
    grad_e,
    w_left,
    w_right,
    w_out,
    w_proj,
    b_left,
    b_right,
    part_a,
    held_a,
    line_a,
    full_a,
    part_b,
    held_b,
    line_b,
    full_b,
    sems,
):
    row, col = lax.axis_index("row"), lax.axis_index("col")
    me = row * cols + col
    channels = rows * cols
    tiles, half_lanes = pair.shape[0] // 2, pair.shape[1]
    width, part_tiles, per = 2 * half_lanes, tiles // PARTS, rows // cols
    strip = rows * part_tiles
    order = sorted(range(cols), key=lambda step: min(step, cols - step))
    barrier = pltpu.get_barrier_semaphore()

    fetches = [
        pltpu.make_async_copy(source, target, in_sems.at[n])
        for n, (source, target) in enumerate(
            (
                (pair_in, pair),
                (right_proj_in, right_proj),
                (right_gate_in, right_gate),
                (pad_in, pad_mask),
                (left_proj_in, left_proj),
                (left_gate_in, left_gate),
                (crop_in, crop_mask),
                (out_gate_in, out_gate),
                (out_proj_in, out_proj),
                (cot_in, cot),
            )
        )
    ]
    for fetch in fetches:
        fetch.start()

    def device(r, c):
        return {"row": r, "col": c}

    def for_rows(act, itself):
        def step(shift, carry):
            act(lax.rem(row + shift, rows))
            return carry

        lax.fori_loop(0 if itself else 1, rows, step, 0)

    def for_peers(act):
        def step(shift, carry):
            for hop in order[1:]:
                act(lax.rem(row + shift, rows), lax.rem(col + hop, cols))

            @pl.when(shift > 0)
            def _():
                act(lax.rem(row + shift, rows), col)

            return carry

        lax.fori_loop(0, rows, step, 0)

    for_peers(
        lambda r, c: pl.semaphore_signal(
            barrier, inc=1, device_id=device(r, c), device_id_type=MESH
        )
    )

    def copy_to(src, dst, which, r, c):
        pltpu.make_async_remote_copy(
            src_ref=src,
            dst_ref=dst,
            send_sem=sems.at[2 * which],
            recv_sem=sems.at[2 * which + 1],
            device_id=device(r, c),
            device_id_type=MESH,
        ).start()

    def to_owners(src, dst, which, part):
        dst[part, col, row] = src[part, me]
        for_peers(
            lambda r, c: copy_to(
                src.at[part, r * cols + c], dst.at[part, col, row], which + part, r, c
            )
        )

    def from_owner(src, dst, which, part, r, c):
        copy_to(src.at[part, c, r], dst.at[part, me], which + part, r, c)

    def keep_own(src, dst, part):
        dst[part, me] = src[part, col, row]

    def arrived(which, part):
        wait_bytes(send_l.at[0, pl.ds(0, channels - 1)], sems.at[2 * (which + part) + 1])

    def sent(which):
        wait_bytes(send_l.at[0, pl.ds(0, channels - 1)], sems.at[2 * which])

    def for_tiles(part, body):
        def step(q, carry):
            body(part * part_tiles + q, q)
            return carry

        lax.fori_loop(0, part_tiles, step, 0, unroll=2)

    def lanes(p):
        return pl.ds(pl.multiple_of(p * width, width), width)

    def strided(q):
        return pl.ds(q, channels, stride=part_tiles)

    def part_lanes(part):
        return pl.ds(part * part_tiles * width, part_tiles * width)

    def pack(dst, part):
        dst[part] = stage[...].reshape(channels, part_tiles, width).astype(BF16)

    def unpack(src, part):
        stage[...] = src[part].astype(F32).reshape(channels * part_tiles, width)

    lane = lax.broadcasted_iota(jnp.int32, (1, width), 1)
    low = lane < half_lanes

    def mask_of(ref):
        def put(n, line):
            value = ref[col * half_lanes + n].astype(F32)
            hit = jnp.logical_or(lane == n, lane == n + half_lanes)
            return jnp.where(hit, value, line)

        line = lax.fori_loop(0, half_lanes, put, jnp.zeros((1, width), F32), unroll=4)

        def mask(p):
            first = ref[row * 2 * tiles + p].astype(F32)
            second = ref[row * 2 * tiles + tiles + p].astype(F32)
            return jnp.where(low, first, second) * line

        return mask

    def tile_t(ref, p):
        both = jnp.concatenate([ref[p], ref[p + tiles]], axis=0)
        return both.astype(F32).T

    def put_tile(ref, p, values):
        back = values.T.astype(BF16)
        ref[p] = back[:half_lanes]
        ref[p + tiles] = back[half_lanes:]

    def flip(ref):
        return ref[...].astype(F32).T.astype(BF16)

    size = left_proj.shape[0]
    for fetch in fetches[:4]:
        fetch.wait()
    w_right[:size] = flip(right_proj)
    w_right[size:] = flip(right_gate)
    pad = mask_of(pad_mask)

    def edge(p, q, normed, weight, value_ref, sig_ref):
        both = dot_nn(weight[...], normed)
        value, sig = both[:size], jax.nn.sigmoid(both[size:])
        value_ref[p] = value
        sig_ref[p] = sig
        stage[strided(q), :] = pad(p) * sig * value

    def right_tile(p, q):
        wide = tile_t(pair, p)
        center = wide - mean_rows(wide)
        rstd = lax.rsqrt(mean_rows(center * center) + EPS)
        hat = center * rstd
        xhat[p] = hat
        scale[p] = rstd
        normed = hat.astype(BF16)
        norm_t[:, lanes(p)] = normed
        edge(p, q, normed, w_right, right_v, right_s)

    def left_tile(p, q):
        edge(p, q, norm_t[:, lanes(p)], w_left, left_v, left_s)

    for part in range(PARTS):
        for_tiles(part, right_tile)
        pack(send_r, part)
        if part == 0:
            pl.semaphore_wait(barrier, channels - 1)
        to_owners(send_r, recv_r, RIGHT, part)
    for fetch in fetches[4:]:
        fetch.wait()
    w_left[:size] = flip(left_proj)
    w_left[size:] = flip(left_gate)
    for part in range(PARTS):
        for_tiles(part, left_tile)
        pack(send_l, part)
        to_owners(send_l, recv_l, LEFT, part)

    w_out[...] = flip(out_gate)
    w_proj[...] = flip(out_proj)
    b_left[:, :size] = left_proj[...]
    b_left[:, size:] = left_gate[...]
    b_right[:, :size] = right_proj[...]
    b_right[:, size:] = right_gate[...]
    crop = mask_of(crop_mask)

    def out_tile(p, q):
        gate = jax.nn.sigmoid(dot_nn(w_out[...], norm_t[:, lanes(p)]))
        upstream = crop(p) * tile_t(cot, p)
        projected_grad = (upstream * gate).astype(BF16)
        grad_p[:, lanes(p)] = projected_grad
        gate_c[p] = crop(p) * gate
        gate_u[p] = upstream * gate * (1.0 - gate)
        grad_ns[p] = dot_nn(out_proj[...], projected_grad)

    for part in range(PARTS):
        for_tiles(part, out_tile)

    for part in range(PARTS):
        arrived(RIGHT, part)

    def spread_block(k, carry):
        for c in range(cols):
            raw = recv_r[:, k, c * per : (c + 1) * per].astype(F32)
            turned = pltpu.roll(raw.reshape(PARTS * per * part_tiles, width), half_lanes, 1)
            turned = turned.reshape(raw.shape)
            pieces = []
            for half in range(2):
                for r in range(per):
                    for own in range(2):
                        for part in range(PARTS):
                            piece = raw[part, r] if half == own else turned[part, r]
                            keep = low if half == 0 else jnp.logical_not(low)
                            pieces.append(jnp.where(keep, piece, 0.0))
            block = jnp.concatenate(pieces, axis=0).astype(BF16)
            spread[c * width : (c + 1) * width, lanes(k)] = block
        return carry

    lax.fori_loop(0, cols, spread_block, 0)

    def gather(src, dst, part):
        for c in range(cols):
            block = src[part, c].astype(F32).reshape(strip, width).astype(BF16)
            dst[part * strip : (part + 1) * strip, c * width : (c + 1) * width] = block

    def send_strip(src, dst, which, part, hop, c, values):
        src[part, c] = values.reshape(rows, part_tiles, width).astype(BF16)
        for_rows(lambda r: from_owner(src, dst, which, part, r, c), hop != 0)

    def strip_of(mat, part):
        return mat[part * strip : (part + 1) * strip, :]

    hops = order[1:] + order[:1]
    for part in range(PARTS):
        arrived(LEFT, part)
        gather(recv_l, mat_l, part)
        for hop in hops:
            c = lax.rem(col + hop, cols)
            sums = dot_nt(strip_of(mat_l, part), spread[lanes(c), :])
            send_strip(send_s, recv_s, SUMS, part, hop, c, sums)
        keep_own(send_s, recv_s, part)

    def sum_tile(p, q):
        sums = stage[strided(q), :]
        center = sums - mean_rows(sums)
        rstd = lax.rsqrt(mean_rows(center * center) + EPS)
        hat = center * rstd
        norm_s[:, lanes(p)] = hat.astype(BF16)
        grad = grad_ns[p]
        grad = rstd * (grad - mean_rows(grad) - hat * mean_rows(grad * hat))
        stage[strided(q), :] = grad

    for part in range(PARTS):
        arrived(SUMS, part)
        unpack(recv_s, part)
        for_tiles(part, sum_tile)
        pack(send_g, part)
        to_owners(send_g, recv_g, GRADS, part)

    def result_tile(p, q):
        projected = dot_nn(w_proj[...], norm_s[:, lanes(p)])
        put_tile(result, p, gate_c[p] * projected)
        logit = (gate_u[p] * projected).astype(BF16)
        grad_o[:, lanes(p)] = logit
        grad_n[p] = dot_nn(out_gate[...], logit)

    for part in range(PARTS):
        for_tiles(part, result_tile)
        arrived(GRADS, part)
        gather(recv_g, mat_g, part)
        for hop in hops:
            c = lax.rem(col + hop, cols)
            grads = dot_nn(strip_of(mat_g, part), spread[:, lanes(c)])
            send_strip(send_dl, recv_dl, LEFT_GRADS, part, hop, c, grads)
        keep_own(send_dl, recv_dl, part)

    def right_block(c, carry):
        outer = dot_tn(mat_g[:, lanes(c)], mat_l[...])
        for k in range(cols):
            block = outer[:, k * width : (k + 1) * width]
            block = block.reshape(2, per, 2, tiles, width)
            keep = jnp.where(low, block[0, :, 0], block[1, :, 1])
            turn = jnp.where(low, block[0, :, 1], block[1, :, 0])
            turn = pltpu.roll(turn.reshape(per * tiles, width), half_lanes, 1)
            total = (keep.reshape(per * tiles, width) + turn).reshape(
                per, PARTS, part_tiles, width
            )
            for part in range(PARTS):
                send_dr[part, k, pl.ds(c * per, per)] = total[:, part].astype(BF16)
        return carry

    lax.fori_loop(0, cols, right_block, 0)
    for part in range(PARTS):
        for_peers(lambda r, c: from_owner(send_dr, recv_dr, RIGHT_GRADS, part, r, c))
        keep_own(send_dr, recv_dr, part)

    inverse = 1.0 / (rows * 2 * tiles)

    def put_weight(ref, place, values):
        high = size // rows
        ref[:, place * high : (place + 1) * high, :] = (values * inverse).reshape(
            rows, high, size
        )

    def weight_parts(part, held, which):
        held[row] = part[row]
        for_rows(lambda r: copy_to(part.at[r], held.at[row], which, r, col), False)

    def weight_lines(held, line, which):
        wait_bytes(held.at[pl.ds(0, rows - 1)], sems.at[2 * which + 1])
        line[col] = jnp.sum(held[...], axis=0)
        for hop in order[1:]:
            copy_to(line.at[col], line.at[col], which + 1, row, lax.rem(col + hop, cols))

    def weight_full(line, full, which):
        wait_bytes(line.at[pl.ds(0, cols - 1)], sems.at[2 * which + 3])
        full[row] = jnp.sum(line[...], axis=0)
        for_rows(lambda r: copy_to(full.at[row], full.at[row], which + 2, r, col), False)

    def weight_done(line, full, which, places):
        wait_bytes(full.at[pl.ds(0, rows - 1)], sems.at[2 * which + 5])
        high = size // rows
        for slot, place in enumerate(places):
            part = full[:, slot * high : (slot + 1) * high, :]
            weight_grads[place] = part.reshape(size, size)
        wait_bytes(full.at[pl.ds(0, rows - 1)], sems.at[2 * which])
        wait_bytes(line.at[pl.ds(0, cols - 1)], sems.at[2 * which + 2])
        wait_bytes(full.at[pl.ds(0, rows - 1)], sems.at[2 * which + 4])

    def edge_grads(p, q, value_ref, sig_ref):
        grad, sig = pad(p) * stage[strided(q), :], sig_ref[p]
        grad_v = grad * sig
        grad_e[:size, lanes(p)] = grad_v.astype(BF16)
        grad_e[size:, lanes(p)] = (grad_v * value_ref[p] * (1.0 - sig)).astype(BF16)

    def left_back(p, q):
        edge_grads(p, q, left_v, left_s)
        grad_n[p] += dot_nn(b_left[...], grad_e[:, lanes(p)])

    def right_back(p, q):
        edge_grads(p, q, right_v, right_s)

    def edge_weights(part):
        return dot_nt(norm_t[:, part_lanes(part)], grad_e[:, part_lanes(part)])

    def pair_tile(p, q):
        grad = grad_n[p] + dot_nn(b_right[...], grad_e[:, lanes(p)])
        hat = xhat[p]
        grad = scale[p] * (grad - mean_rows(grad) - hat * mean_rows(grad * hat))
        put_tile(grad_pair, p, grad)

    put_weight(part_a, 2, dot_nt(norm_t[...], grad_o[...]))
    put_weight(part_a, 3, dot_nt(norm_s[...], grad_p[...]))
    total = None
    for part in range(PARTS):
        arrived(LEFT_GRADS, part)
        unpack(recv_dl, part)
        for_tiles(part, left_back)
        both = edge_weights(part)
        total = both if part == 0 else total + both
    put_weight(part_a, 0, total[:, :size])
    put_weight(part_a, 1, total[:, size:])
    weight_parts(part_a, held_a, WEIGHTS_A)
    for part in range(PARTS):
        arrived(RIGHT_GRADS, part)
        unpack(recv_dr, part)
        for_tiles(part, right_back)
        both = edge_weights(part)
        total = both if part == 0 else total + both
        if part < PARTS - 1:
            for_tiles(part, pair_tile)
            weight_lines(held_a, line_a, WEIGHTS_A)
    put_weight(part_b, 0, total[:, :size])
    put_weight(part_b, 1, total[:, size:])
    weight_parts(part_b, held_b, WEIGHTS_B)
    weight_full(line_a, full_a, WEIGHTS_A)
    weight_lines(held_b, line_b, WEIGHTS_B)
    for_tiles(PARTS - 1, pair_tile)
    weight_full(line_b, full_b, WEIGHTS_B)
    weight_done(line_a, full_a, WEIGHTS_A, (0, 1, 4, 5))
    weight_done(line_b, full_b, WEIGHTS_B, (2, 3))
    for which in range(6 * PARTS):
        sent(which)


def shards(
    pair,
    pad_mask,
    crop_mask,
    left_proj,
    left_gate,
    right_proj,
    right_gate,
    out_gate,
    out_proj,
    cotangent,
):
    rows, cols = lax.axis_size("row"), lax.axis_size("col")
    high, wide, size = pair.shape
    tiles, width, channels = high // 2, 2 * wide, rows * cols
    positions = tiles * width
    vmem = pl.BlockSpec(memory_space=pltpu.VMEM)
    hbm = pl.BlockSpec(memory_space=pltpu.HBM)
    at_home = pltpu.VMEM((PARTS, channels, tiles // PARTS, width), BF16)
    at_owner = pltpu.VMEM((PARTS, cols, rows, tiles // PARTS, width), BF16)
    wide_tiles = pltpu.VMEM((tiles, size, width), F32)
    flat = pltpu.VMEM((size, positions), BF16)
    pair_weights = pltpu.VMEM((2 * size, size), BF16)
    weight = pltpu.VMEM((size, size), BF16)
    back_weights = pltpu.VMEM((size, 2 * size), BF16)
    share = size // rows

    def sum_buffers(count):
        return [
            pltpu.VMEM((rows, count * share, size), F32),
            pltpu.VMEM((rows, count * share, size), F32),
            pltpu.VMEM((cols, count * share, size), F32),
            pltpu.VMEM((rows, count * share, size), F32),
        ]

    return pl.pallas_call(
        functools.partial(kernel, rows, cols),
        out_shape=(
            jax.ShapeDtypeStruct(pair.shape, BF16),
            jax.ShapeDtypeStruct(pair.shape, BF16),
            jax.ShapeDtypeStruct((6, size, size), F32),
        ),
        in_specs=[hbm] * 10,
        out_specs=(vmem, vmem, vmem),
        scratch_shapes=[
            pltpu.VMEM(pair.shape, BF16),
            pltpu.VMEM(pair.shape, BF16),
            pltpu.SMEM(pad_mask.shape, jnp.int32),
            pltpu.SMEM(pad_mask.shape, jnp.int32),
            *[weight] * 6,
            pltpu.SemaphoreType.DMA((10,)),
            at_home,
            at_home,
            at_owner,
            at_home,
            at_owner,
            at_owner,
            at_owner,
            at_owner,
            at_home,
            at_owner,
            at_home,
            at_home,
            pltpu.VMEM((channels * tiles // PARTS, width), F32),
            pltpu.VMEM((cols * width, cols * width), BF16),
            pltpu.VMEM((rows * tiles, cols * width), BF16),
            pltpu.VMEM((rows * tiles, cols * width), BF16),
            flat,
            wide_tiles,
            pltpu.VMEM((tiles, 1, width), F32),
            wide_tiles,
            wide_tiles,
            wide_tiles,
            wide_tiles,
            wide_tiles,
            wide_tiles,
            wide_tiles,
            wide_tiles,
            flat,
            flat,
            flat,
            pltpu.VMEM((2 * size, positions), BF16),
            pair_weights,
            pair_weights,
            weight,
            weight,
            back_weights,
            back_weights,
            *sum_buffers(4),
            *sum_buffers(2),
            pltpu.SemaphoreType.DMA((2 * (WEIGHTS_B + 3),)),
        ],
        compiler_params=pltpu.CompilerParams(
            collective_id=1, has_side_effects=True, vmem_limit_bytes=50 * 2**20
        ),
        name="triangle",
    )(
        pair,
        cotangent,
        pad_mask,
        crop_mask,
        left_proj,
        left_gate,
        right_proj,
        right_gate,
        out_gate,
        out_proj,
    )


def solution(mesh):
    blocks = P(("rep", "row"), "col", None)
    return jax.shard_map(
        shards,
        mesh=mesh,
        in_specs=(blocks, P("rep"), P("rep"), P(), P(), P(), P(), P(), P(), blocks),
        out_specs=(blocks, blocks, P("rep", None, None)),
        check_vma=False,
    )
```

time: 138 us -> 113 us (0.82)
  Pallas kernels: 127 us -> 102 us
    pallas_call x1, Pallas kernels: 127 us -> 102 us  [shards(): pl.pallas_call(functools.partial(kernel, rows, cols), out_shape=(jax.Shap...]
where the time goes in v3:
time: 113 us
  Pallas kernels  102 us (90%)
  local copies, waits for them, and re-layouts  10.3 us (9%)
    pallas_call x1, Pallas kernels, shards(): pl.pallas_call(functools.partial(kernel, rows, cols), out_shape=(jax.Shap...  102 us
    unnamed x23, local copies, waits for them, and re-layouts  10.3 us

profile of v3, /device:TPU:1, one launch (start us, length us, event | category | flops | bytes accessed | tf_op | source)
XLA Modules:
  0.0 112.7 jit_solution(6275444874346861004)
XLA Ops:
  0.6 0.0 copy-start
  0.6 1.0 copy-done
  1.7 0.0 copy-start.1
  1.7 1.0 copy-done.1
  2.7 0.0 copy-start.2
  2.7 0.8 copy-done.2
  3.5 0.0 copy-start.3
  3.5 0.8 copy-done.3
  4.2 0.0 copy-start.4
  4.2 0.8 copy-done.4
  5.0 0.0 copy-start.5
  5.0 0.8 copy-done.5
  5.8 0.0 copy-start.6
  5.8 0.8 copy-done.6
  6.5 0.0 copy-start.7
  6.5 0.8 copy-done.7
  7.3 0.0 copy-start.8
  7.3 0.7 copy-done.8
  8.0 0.0 copy-start.9
  8.0 0.7 copy-done.9
  8.6 101.7 %triangle.1 = (bf16[32,64,128]{2,1,0:T(8,128)(2,1)S(1)}, bf16[32,64,128]{2,1,0:T(8,128)(2,1)S(1)}, f32[6,128,128]{2,1,0:T(8,128)S(1)}) custom-call(bf16[32,64,128]{2,1,0:T(8,128)(2,1)S(1)} %copy-done, bf16[32,64,128]{2,1,0:T(8,128)(2,1)S(1)} %copy-done.1, s32[512]{0:T(512)S(1)} %copy-done.8, s32[512]{0:T(512)S(1)} %copy-done.9, ...), custom_call_target="tpu_custom_call" | custom-call | tf_op jit(solution)/shard_map/triangle/pallas_call | solution.py:538
  110.3 0.8 copy.16
  111.1 0.8 copy.17
  111.9 0.7 copy.18
Async XLA Ops:
  0.6 1.0 copy-start
  1.7 1.0 copy-start.1
  2.7 0.8 copy-start.2
  3.5 0.8 copy-start.3
  4.2 0.8 copy-start.4
  5.0 0.8 copy-start.5
  5.8 0.8 copy-start.6
  6.5 0.8 copy-start.7
  7.3 0.7 copy-start.8
  8.0 0.7 copy-start.9

commit v4 on v3

--- a/solution.py
+++ b/solution.py
@@ -12,6 +12,7 @@
 BF16 = jnp.bfloat16
 EPS = 1e-05
 PARTS = 2
+VMEM_BYTES = 60 * 2**20
 LEFT, RIGHT, SUMS, GRADS, LEFT_GRADS, RIGHT_GRADS = (PARTS * n for n in range(6))
 WEIGHTS_A, WEIGHTS_B = 6 * PARTS, 6 * PARTS + 3
 
@@ -49,6 +50,9 @@
     right_gate_in,
     out_gate_in,
     out_proj_in,
+    result_out,
+    grad_pair_out,
+    weight_grads_out,
     result,
     grad_pair,
     weight_grads,
@@ -63,6 +67,7 @@
     out_gate,
     out_proj,
     in_sems,
+    out_sems,
     send_l,
     send_r,
     send_s,
@@ -138,6 +143,16 @@
     ]
     for fetch in fetches:
         fetch.start()
+    stores = [
+        pltpu.make_async_copy(source, target, out_sems.at[n])
+        for n, (source, target) in enumerate(
+            (
+                (result, result_out),
+                (grad_pair, grad_pair_out),
+                (weight_grads, weight_grads_out),
+            )
+        )
+    ]
 
     def device(r, c):
         return {"row": r, "col": c}
@@ -411,6 +426,8 @@
         for_peers(lambda r, c: from_owner(send_dr, recv_dr, RIGHT_GRADS, part, r, c))
         keep_own(send_dr, recv_dr, part)
 
+    stores[0].start()
+
     inverse = 1.0 / (rows * 2 * tiles)
 
     def put_weight(ref, place, values):
@@ -493,11 +510,49 @@
     weight_full(line_a, full_a, WEIGHTS_A)
     weight_lines(held_b, line_b, WEIGHTS_B)
     for_tiles(PARTS - 1, pair_tile)
+    stores[1].start()
     weight_full(line_b, full_b, WEIGHTS_B)
     weight_done(line_a, full_a, WEIGHTS_A, (0, 1, 4, 5))
     weight_done(line_b, full_b, WEIGHTS_B, (2, 3))
+    stores[2].start()
     for which in range(6 * PARTS):
         sent(which)
+    for store in stores:
+        store.wait()
+
+
+def settle_kernel(count, *refs):
+    arrays, outs, held, sems = refs[:count], refs[count : 2 * count], refs[2 * count : -1], refs[-1]
+    loads = [
+        pltpu.make_async_copy(arrays[n], held[n], sems.at[n]) for n in range(count)
+    ]
+    stores = [
+        pltpu.make_async_copy(held[n], outs[n], sems.at[count + n]) for n in range(count)
+    ]
+    for load in loads:
+        load.start()
+    for load, store in zip(loads, stores):
+        load.wait()
+        store.start()
+    for store in stores:
+        store.wait()
+
+
+def settle(arrays):
+    count = len(arrays)
+    hbm = pl.BlockSpec(memory_space=pltpu.HBM)
+    return pl.pallas_call(
+        functools.partial(settle_kernel, count),
+        out_shape=tuple(jax.ShapeDtypeStruct(a.shape, a.dtype) for a in arrays),
+        in_specs=[hbm] * count,
+        out_specs=(hbm,) * count,
+        scratch_shapes=[
+            *[pltpu.VMEM(a.shape, a.dtype) for a in arrays],
+            pltpu.SemaphoreType.DMA((2 * count,)),
+        ],
+        compiler_params=pltpu.CompilerParams(vmem_limit_bytes=VMEM_BYTES),
+        name="settle",
+    )(*arrays)
 
 
 def shards(
@@ -516,7 +571,6 @@
     high, wide, size = pair.shape
     tiles, width, channels = high // 2, 2 * wide, rows * cols
     positions = tiles * width
-    vmem = pl.BlockSpec(memory_space=pltpu.VMEM)
     hbm = pl.BlockSpec(memory_space=pltpu.HBM)
     at_home = pltpu.VMEM((PARTS, channels, tiles // PARTS, width), BF16)
     at_owner = pltpu.VMEM((PARTS, cols, rows, tiles // PARTS, width), BF16)
@@ -535,7 +589,7 @@
             pltpu.VMEM((rows, count * share, size), F32),
         ]
 
-    return pl.pallas_call(
+    outs = pl.pallas_call(
         functools.partial(kernel, rows, cols),
         out_shape=(
             jax.ShapeDtypeStruct(pair.shape, BF16),
@@ -543,14 +597,18 @@
             jax.ShapeDtypeStruct((6, size, size), F32),
         ),
         in_specs=[hbm] * 10,
-        out_specs=(vmem, vmem, vmem),
+        out_specs=(hbm, hbm, hbm),
         scratch_shapes=[
+            pltpu.VMEM(pair.shape, BF16),
+            pltpu.VMEM(pair.shape, BF16),
+            pltpu.VMEM((6, size, size), F32),
             pltpu.VMEM(pair.shape, BF16),
             pltpu.VMEM(pair.shape, BF16),
             pltpu.SMEM(pad_mask.shape, jnp.int32),
             pltpu.SMEM(pad_mask.shape, jnp.int32),
             *[weight] * 6,
             pltpu.SemaphoreType.DMA((10,)),
+            pltpu.SemaphoreType.DMA((3,)),
             at_home,
             at_home,
             at_owner,
@@ -593,7 +651,7 @@
             pltpu.SemaphoreType.DMA((2 * (WEIGHTS_B + 3),)),
         ],
         compiler_params=pltpu.CompilerParams(
-            collective_id=1, has_side_effects=True, vmem_limit_bytes=50 * 2**20
+            collective_id=1, has_side_effects=True, vmem_limit_bytes=VMEM_BYTES
         ),
         name="triangle",
     )(
@@ -608,6 +666,7 @@
         out_gate,
         out_proj,
     )
+    return settle(outs)
 
 
 def solution(mesh):

time: 113 us -> 105 us (0.929)
  local copies, waits for them, and re-layouts: 10.3 us -> 0 us
  Pallas kernels: 102 us -> 105 us
    unnamed x23 -> x0, local copies, waits for them, and re-layouts: 10.3 us -> none
    pallas_call x0 -> x1, Pallas kernels: none -> 2.18 us  [settle(): pl.pallas_call(functools.partial(settle_kernel, count), out_shape=tuple((...]
where the time goes in v4:
time: 105 us
  Pallas kernels  105 us (100%)
    pallas_call x1, Pallas kernels, shards(): pl.pallas_call(functools.partial(kernel, rows, cols), out_shape=(jax.Shap...  102 us
    pallas_call x1, Pallas kernels, settle(): pl.pallas_call(functools.partial(settle_kernel, count), out_shape=tuple((...  2.18 us

profile of v4, /device:TPU:1, one launch (start us, length us, event | category | flops | bytes accessed | tf_op | source)
XLA Modules:
  0.0 105.3 jit_solution(13722862220289553561)
XLA Ops:
  0.6 102.4 %triangle.1 = (bf16[32,64,128]{2,1,0:T(8,128)(2,1)}, bf16[32,64,128]{2,1,0:T(8,128)(2,1)}, f32[6,128,128]{2,1,0:T(8,128)}) custom-call(bf16[32,64,128]{2,1,0:T(8,128)(2,1)} %pair_in.1, bf16[32,64,128]{2,1,0:T(8,128)(2,1)} %cot_in.1, s32[512]{0:T(512)} %pad_in.1, s32[512]{0:T(512)} %crop_in.1, bf16[128,128]{1,0:T(8,128)(2,1)} %left_proj_in.1, ...), custom_call_target="tpu_custom_call" | custom-call | tf_op jit(solution)/shard_map/triangle/pallas_call | solution.py:592
  103.1 2.2 %settle.1 = (bf16[32,64,128]{2,1,0:T(8,128)(2,1)}, bf16[32,64,128]{2,1,0:T(8,128)(2,1)}, f32[6,128,128]{2,1,0:T(8,128)}) custom-call(bf16[32,64,128]{2,1,0:T(8,128)(2,1)} %get-tuple-element.6.refs_0_, bf16[32,64,128]{2,1,0:T(8,128)(2,1)} %get-tuple-element.7.refs_1_, f32[6,128,128]{2,1,0:T(8,128)} %get-tuple-element.8.refs_2_), custom_call_target="tpu_custom_call" | custom-call | tf_op jit(solution)/shard_map/settle/pallas_call | solution.py:544

commit v5 on v3

--- a/solution.py
+++ b/solution.py
@@ -12,8 +12,10 @@
 BF16 = jnp.bfloat16
 EPS = 1e-05
 PARTS = 2
+VMEM_BYTES = 50 * 2**20
+SETTLE_BYTES = 4 * 2**20
 LEFT, RIGHT, SUMS, GRADS, LEFT_GRADS, RIGHT_GRADS = (PARTS * n for n in range(6))
-WEIGHTS_A, WEIGHTS_B = 6 * PARTS, 6 * PARTS + 3
+WEIGHTS_O, WEIGHTS_L, WEIGHTS_R = (6 * PARTS + 3 * n for n in range(3))
 
 
 def dot_nn(left, right):
@@ -100,14 +102,18 @@
     w_proj,
     b_left,
     b_right,
-    part_a,
-    held_a,
-    line_a,
-    full_a,
-    part_b,
-    held_b,
-    line_b,
-    full_b,
+    part_o,
+    held_o,
+    line_o,
+    full_o,
+    part_l,
+    held_l,
+    line_l,
+    full_l,
+    part_r,
+    held_r,
+    line_r,
+    full_r,
     sems,
 ):
     row, col = lax.axis_index("row"), lax.axis_index("col")
@@ -123,10 +129,10 @@
         pltpu.make_async_copy(source, target, in_sems.at[n])
         for n, (source, target) in enumerate(
             (
-                (pair_in, pair),
                 (right_proj_in, right_proj),
                 (right_gate_in, right_gate),
                 (pad_in, pad_mask),
+                (pair_in, pair),
                 (left_proj_in, left_proj),
                 (left_gate_in, left_gate),
                 (crop_in, crop_mask),
@@ -251,11 +257,12 @@
         return ref[...].astype(F32).T.astype(BF16)
 
     size = left_proj.shape[0]
-    for fetch in fetches[:4]:
+    for fetch in fetches[:3]:
         fetch.wait()
     w_right[:size] = flip(right_proj)
     w_right[size:] = flip(right_gate)
     pad = mask_of(pad_mask)
+    fetches[3].wait()
 
     def edge(p, q, normed, weight, value_ref, sig_ref):
         both = dot_nn(weight[...], normed)
@@ -347,7 +354,7 @@
     def strip_of(mat, part):
         return mat[part * strip : (part + 1) * strip, :]
 
-    hops = order[1:] + order[:1]
+    hops = order[::-1]
     for part in range(PARTS):
         arrived(LEFT, part)
         gather(recv_l, mat_l, part)
@@ -381,8 +388,46 @@
         grad_o[:, lanes(p)] = logit
         grad_n[p] = dot_nn(out_gate[...], logit)
 
+    inverse = 1.0 / (rows * 2 * tiles)
+
+    def put_weight(ref, place, values):
+        high = size // rows
+        ref[:, place * high : (place + 1) * high, :] = (values * inverse).reshape(
+            rows, high, size
+        )
+
+    def weight_parts(part, held, which):
+        held[row] = part[row]
+        for_rows(lambda r: copy_to(part.at[r], held.at[row], which, r, col), False)
+
+    def weight_lines(held, line, which):
+        wait_bytes(held.at[pl.ds(0, rows - 1)], sems.at[2 * which + 1])
+        line[col] = jnp.sum(held[...], axis=0)
+        for hop in order[1:]:
+            copy_to(line.at[col], line.at[col], which + 1, row, lax.rem(col + hop, cols))
+
+    def weight_full(line, full, which):
+        wait_bytes(line.at[pl.ds(0, cols - 1)], sems.at[2 * which + 3])
+        full[row] = jnp.sum(line[...], axis=0)
+        for_rows(lambda r: copy_to(full.at[row], full.at[row], which + 2, r, col), False)
+
+    def weight_store(full, which, places):
+        wait_bytes(full.at[pl.ds(0, rows - 1)], sems.at[2 * which + 5])
+        high = size // rows
+        for slot, place in enumerate(places):
+            weight_grads[place] = full[:, slot * high : (slot + 1) * high, :]
+
+    def weight_sent(line, full, which):
+        wait_bytes(full.at[pl.ds(0, rows - 1)], sems.at[2 * which])
+        wait_bytes(line.at[pl.ds(0, cols - 1)], sems.at[2 * which + 2])
+        wait_bytes(full.at[pl.ds(0, rows - 1)], sems.at[2 * which + 4])
+
     for part in range(PARTS):
         for_tiles(part, result_tile)
+    put_weight(part_o, 0, dot_nt(norm_t[...], grad_o[...]))
+    put_weight(part_o, 1, dot_nt(norm_s[...], grad_p[...]))
+    weight_parts(part_o, held_o, WEIGHTS_O)
+    for part in range(PARTS):
         arrived(GRADS, part)
         gather(recv_g, mat_g, part)
         for hop in hops:
@@ -390,6 +435,8 @@
             grads = dot_nn(strip_of(mat_g, part), spread[:, lanes(c)])
             send_strip(send_dl, recv_dl, LEFT_GRADS, part, hop, c, grads)
         keep_own(send_dl, recv_dl, part)
+        if part == 0:
+            weight_lines(held_o, line_o, WEIGHTS_O)
 
     def right_block(c, carry):
         outer = dot_tn(mat_g[:, lanes(c)], mat_l[...])
@@ -410,39 +457,7 @@
     for part in range(PARTS):
         for_peers(lambda r, c: from_owner(send_dr, recv_dr, RIGHT_GRADS, part, r, c))
         keep_own(send_dr, recv_dr, part)
-
-    inverse = 1.0 / (rows * 2 * tiles)
-
-    def put_weight(ref, place, values):
-        high = size // rows
-        ref[:, place * high : (place + 1) * high, :] = (values * inverse).reshape(
-            rows, high, size
-        )
-
-    def weight_parts(part, held, which):
-        held[row] = part[row]
-        for_rows(lambda r: copy_to(part.at[r], held.at[row], which, r, col), False)
-
-    def weight_lines(held, line, which):
-        wait_bytes(held.at[pl.ds(0, rows - 1)], sems.at[2 * which + 1])
-        line[col] = jnp.sum(held[...], axis=0)
-        for hop in order[1:]:
-            copy_to(line.at[col], line.at[col], which + 1, row, lax.rem(col + hop, cols))
-
-    def weight_full(line, full, which):
-        wait_bytes(line.at[pl.ds(0, cols - 1)], sems.at[2 * which + 3])
-        full[row] = jnp.sum(line[...], axis=0)
-        for_rows(lambda r: copy_to(full.at[row], full.at[row], which + 2, r, col), False)
-
-    def weight_done(line, full, which, places):
-        wait_bytes(full.at[pl.ds(0, rows - 1)], sems.at[2 * which + 5])
-        high = size // rows
-        for slot, place in enumerate(places):
-            part = full[:, slot * high : (slot + 1) * high, :]
-            weight_grads[place] = part.reshape(size, size)
-        wait_bytes(full.at[pl.ds(0, rows - 1)], sems.at[2 * which])
-        wait_bytes(line.at[pl.ds(0, cols - 1)], sems.at[2 * which + 2])
-        wait_bytes(full.at[pl.ds(0, rows - 1)], sems.at[2 * which + 4])
+    weight_full(line_o, full_o, WEIGHTS_O)
 
     def edge_grads(p, q, value_ref, sig_ref):
         grad, sig = pad(p) * stage[strided(q), :], sig_ref[p]
@@ -466,8 +481,6 @@
         grad = scale[p] * (grad - mean_rows(grad) - hat * mean_rows(grad * hat))
         put_tile(grad_pair, p, grad)
 
-    put_weight(part_a, 2, dot_nt(norm_t[...], grad_o[...]))
-    put_weight(part_a, 3, dot_nt(norm_s[...], grad_p[...]))
     total = None
     for part in range(PARTS):
         arrived(LEFT_GRADS, part)
@@ -475,9 +488,9 @@
         for_tiles(part, left_back)
         both = edge_weights(part)
         total = both if part == 0 else total + both
-    put_weight(part_a, 0, total[:, :size])
-    put_weight(part_a, 1, total[:, size:])
-    weight_parts(part_a, held_a, WEIGHTS_A)
+    put_weight(part_l, 0, total[:, :size])
+    put_weight(part_l, 1, total[:, size:])
+    weight_parts(part_l, held_l, WEIGHTS_L)
     for part in range(PARTS):
         arrived(RIGHT_GRADS, part)
         unpack(recv_dr, part)
@@ -486,18 +499,50 @@
         total = both if part == 0 else total + both
         if part < PARTS - 1:
             for_tiles(part, pair_tile)
-            weight_lines(held_a, line_a, WEIGHTS_A)
-    put_weight(part_b, 0, total[:, :size])
-    put_weight(part_b, 1, total[:, size:])
-    weight_parts(part_b, held_b, WEIGHTS_B)
-    weight_full(line_a, full_a, WEIGHTS_A)
-    weight_lines(held_b, line_b, WEIGHTS_B)
+    put_weight(part_r, 0, total[:, :size])
+    put_weight(part_r, 1, total[:, size:])
+    weight_parts(part_r, held_r, WEIGHTS_R)
+    weight_lines(held_l, line_l, WEIGHTS_L)
+    weight_lines(held_r, line_r, WEIGHTS_R)
     for_tiles(PARTS - 1, pair_tile)
-    weight_full(line_b, full_b, WEIGHTS_B)
-    weight_done(line_a, full_a, WEIGHTS_A, (0, 1, 4, 5))
-    weight_done(line_b, full_b, WEIGHTS_B, (2, 3))
+    weight_full(line_l, full_l, WEIGHTS_L)
+    weight_store(full_o, WEIGHTS_O, (4, 5))
+    weight_full(line_r, full_r, WEIGHTS_R)
     for which in range(6 * PARTS):
         sent(which)
+    weight_sent(line_o, full_o, WEIGHTS_O)
+    weight_store(full_l, WEIGHTS_L, (0, 1))
+    weight_sent(line_l, full_l, WEIGHTS_L)
+    weight_store(full_r, WEIGHTS_R, (2, 3))
+    weight_sent(line_r, full_r, WEIGHTS_R)
+
+
+def settle_kernel(count, *refs):
+    arrays, outs, sems = refs[:count], refs[count : 2 * count], refs[-1]
+    moves = [
+        pltpu.make_async_copy(arrays[n], outs[n], sems.at[n]) for n in range(count)
+    ]
+    for move in moves:
+        move.start()
+    for move in moves:
+        move.wait()
+
+
+def settle(arrays):
+    count = len(arrays)
+    hbm = pl.BlockSpec(memory_space=pltpu.HBM)
+    vmem = pl.BlockSpec(memory_space=pltpu.VMEM)
+    return pl.pallas_call(
+        functools.partial(settle_kernel, count),
+        out_shape=tuple(jax.ShapeDtypeStruct(a.shape, a.dtype) for a in arrays),
+        in_specs=[vmem] * count,
+        out_specs=(hbm,) * count,
+        scratch_shapes=[
+            pltpu.SemaphoreType.DMA((count,)),
+        ],
+        compiler_params=pltpu.CompilerParams(vmem_limit_bytes=SETTLE_BYTES),
+        name="settle",
+    )(*arrays)
 
 
 def shards(
@@ -516,8 +561,8 @@
     high, wide, size = pair.shape
     tiles, width, channels = high // 2, 2 * wide, rows * cols
     positions = tiles * width
+    hbm = pl.BlockSpec(memory_space=pltpu.HBM)
     vmem = pl.BlockSpec(memory_space=pltpu.VMEM)
-    hbm = pl.BlockSpec(memory_space=pltpu.HBM)
     at_home = pltpu.VMEM((PARTS, channels, tiles // PARTS, width), BF16)
     at_owner = pltpu.VMEM((PARTS, cols, rows, tiles // PARTS, width), BF16)
     wide_tiles = pltpu.VMEM((tiles, size, width), F32)
@@ -535,12 +580,12 @@
             pltpu.VMEM((rows, count * share, size), F32),
         ]
 
-    return pl.pallas_call(
+    outs = pl.pallas_call(
         functools.partial(kernel, rows, cols),
         out_shape=(
-            jax.ShapeDtypeStruct(pair.shape, BF16),
-            jax.ShapeDtypeStruct(pair.shape, BF16),
-            jax.ShapeDtypeStruct((6, size, size), F32),
+            pltpu.VMEM(pair.shape, BF16),
+            pltpu.VMEM(pair.shape, BF16),
+            pltpu.VMEM((6, rows, share, size), F32),
         ),
         in_specs=[hbm] * 10,
         out_specs=(vmem, vmem, vmem),
@@ -588,26 +633,32 @@
             weight,
             back_weights,
             back_weights,
-            *sum_buffers(4),
-            *sum_buffers(2),
-            pltpu.SemaphoreType.DMA((2 * (WEIGHTS_B + 3),)),
+            *sum_buffers(2) * 3,
+            pltpu.SemaphoreType.DMA((2 * (WEIGHTS_R + 3),)),
         ],
         compiler_params=pltpu.CompilerParams(
-            collective_id=1, has_side_effects=True, vmem_limit_bytes=50 * 2**20
+            collective_id=1, has_side_effects=True, vmem_limit_bytes=VMEM_BYTES
         ),
         name="triangle",
     )(
-        pair,
-        cotangent,
-        pad_mask,
-        crop_mask,
-        left_proj,
-        left_gate,
-        right_proj,
-        right_gate,
-        out_gate,
-        out_proj,
+        *[
+            pltpu.with_memory_space_constraint(array, pltpu.HBM)
+            for array in (
+                pair,
+                cotangent,
+                pad_mask,
+                crop_mask,
+                left_proj,
+                left_gate,
+                right_proj,
+                right_gate,
+                out_gate,
+                out_proj,
+            )
+        ]
     )
+    result, grad_pair, weight_grads = settle(outs)
+    return result, grad_pair, weight_grads.reshape(6, size, size)
 
 
 def solution(mesh):

time: 113 us -> 103 us (0.912)
  local copies, waits for them, and re-layouts: 10.3 us -> 0 us
    unnamed x23 -> x0, local copies, waits for them, and re-layouts: 10.3 us -> none
    pallas_call x1 -> x2, Pallas kernels: 102 us -> 102 us  [the longest x1 101 us: shards(): pl.pallas_call(functools.partial(kernel, rows, cols), out_shape=(pltpu.VM...]
where the time goes in v5:
time: 103 us
  Pallas kernels  102 us (99%)
    pallas_call x1, Pallas kernels, shards(): pl.pallas_call(functools.partial(kernel, rows, cols), out_shape=(pltpu.VM...  101 us

profile of v5, /device:TPU:1, one launch (start us, length us, event | category | flops | bytes accessed | tf_op | source)
XLA Modules:
  0.0 102.7 jit_solution(5973016023706262210)
XLA Ops:
  0.6 101.0 %triangle.1 = (bf16[32,64,128]{2,1,0:T(8,128)(2,1)S(1)}, bf16[32,64,128]{2,1,0:T(8,128)(2,1)S(1)}, f32[6,16,8,128]{3,2,1,0:T(8,128)S(1)}) custom-call(bf16[32,64,128]{2,1,0:T(8,128)(2,1)} %pair_in.1, bf16[32,64,128]{2,1,0:T(8,128)(2,1)} %cot_in.1, s32[512]{0:T(512)} %pad_in.1, s32[512]{0:T(512)} %crop_in.1, bf16[128,128]{1,0:T(8,128)(2,1)} %left_proj_in.1, ...), custom_call_target="tpu_custom_call" | custom-call | tf_op jit(solution)/shard_map/triangle/pallas_call | solution.py:583
  101.6 1.1 %settle.1 = (bf16[32,64,128]{2,1,0:T(8,128)(2,1)}, bf16[32,64,128]{2,1,0:T(8,128)(2,1)}, f32[6,16,8,128]{3,2,1,0:T(8,128)}) custom-call(bf16[32,64,128]{2,1,0:T(8,128)(2,1)S(1)} %get-tuple-element.9.refs_0_, bf16[32,64,128]{2,1,0:T(8,128)(2,1)S(1)} %get-tuple-element.10.refs_1_, f32[6,16,8,128]{3,2,1,0:T(8,128)S(1)} %get-tuple-element.11.refs_2_), custom_call_target="tpu_custom_call" | custom-call | tf_op jit(solution)/shard_map/settle/pallas_call | solution.py:535

commit v6 on v5

--- a/solution.py
+++ b/solution.py
@@ -157,7 +157,7 @@
 
     def for_peers(act):
         def step(shift, carry):
-            for hop in order[1:]:
+            for hop in order[:0:-1]:
                 act(lax.rem(row + shift, rows), lax.rem(col + hop, cols))
 
             @pl.when(shift > 0)
@@ -209,7 +209,7 @@
             body(part * part_tiles + q, q)
             return carry
 
-        lax.fori_loop(0, part_tiles, step, 0, unroll=2)
+        lax.fori_loop(0, part_tiles, step, 0, unroll=8)
 
     def lanes(p):
         return pl.ds(pl.multiple_of(p * width, width), width)
@@ -403,7 +403,7 @@
     def weight_lines(held, line, which):
         wait_bytes(held.at[pl.ds(0, rows - 1)], sems.at[2 * which + 1])
         line[col] = jnp.sum(held[...], axis=0)
-        for hop in order[1:]:
+        for hop in order[:0:-1]:
             copy_to(line.at[col], line.at[col], which + 1, row, lax.rem(col + hop, cols))
 
     def weight_full(line, full, which):

time: 103 us -> 102 us (level)
  no operation moved by 1% of the time
where the time goes in v6:
time: 102 us
  Pallas kernels  101 us (99%)
    pallas_call x1, Pallas kernels, shards(): pl.pallas_call(functools.partial(kernel, rows, cols), out_shape=(pltpu.VM...  100 us

profile of v6, /device:TPU:1, one launch (start us, length us, event | category | flops | bytes accessed | tf_op | source)
XLA Modules:
  0.0 101.7 jit_solution(1306307471805471437)
XLA Ops:
  0.6 100.0 %triangle.1 = (bf16[32,64,128]{2,1,0:T(8,128)(2,1)S(1)}, bf16[32,64,128]{2,1,0:T(8,128)(2,1)S(1)}, f32[6,16,8,128]{3,2,1,0:T(8,128)S(1)}) custom-call(bf16[32,64,128]{2,1,0:T(8,128)(2,1)} %pair_in.1, bf16[32,64,128]{2,1,0:T(8,128)(2,1)} %cot_in.1, s32[512]{0:T(512)} %pad_in.1, s32[512]{0:T(512)} %crop_in.1, bf16[128,128]{1,0:T(8,128)(2,1)} %left_proj_in.1, ...), custom_call_target="tpu_custom_call" | custom-call | tf_op jit(solution)/shard_map/triangle/pallas_call | solution.py:583
  100.6 1.1 %settle.1 = (bf16[32,64,128]{2,1,0:T(8,128)(2,1)}, bf16[32,64,128]{2,1,0:T(8,128)(2,1)}, f32[6,16,8,128]{3,2,1,0:T(8,128)}) custom-call(bf16[32,64,128]{2,1,0:T(8,128)(2,1)S(1)} %get-tuple-element.9.refs_0_, bf16[32,64,128]{2,1,0:T(8,128)(2,1)S(1)} %get-tuple-element.10.refs_1_, f32[6,16,8,128]{3,2,1,0:T(8,128)S(1)} %get-tuple-element.11.refs_2_), custom_call_target="tpu_custom_call" | custom-call | tf_op jit(solution)/shard_map/settle/pallas_call | solution.py:535

commit v7 on v6

--- a/solution.py
+++ b/solution.py
@@ -315,7 +315,13 @@
         grad_p[:, lanes(p)] = projected_grad
         gate_c[p] = crop(p) * gate
         gate_u[p] = upstream * gate * (1.0 - gate)
-        grad_ns[p] = dot_nn(out_proj[...], projected_grad)
+        back = dot_nn(out_proj[...], projected_grad)
+        grad_ns[p] = back - mean_rows(back)
+        for value_ref, sig_ref in ((left_v, left_s), (right_v, right_s)):
+            sig = sig_ref[p]
+            slope = pad(p) * sig
+            value_ref[p] = slope * value_ref[p] * (1.0 - sig)
+            sig_ref[p] = slope
 
     for part in range(PARTS):
         for_tiles(part, out_tile)
@@ -371,7 +377,7 @@
         hat = center * rstd
         norm_s[:, lanes(p)] = hat.astype(BF16)
         grad = grad_ns[p]
-        grad = rstd * (grad - mean_rows(grad) - hat * mean_rows(grad * hat))
+        grad = rstd * (grad - hat * mean_rows(grad * hat))
         stage[strided(q), :] = grad
 
     for part in range(PARTS):
@@ -460,10 +466,9 @@
     weight_full(line_o, full_o, WEIGHTS_O)
 
     def edge_grads(p, q, value_ref, sig_ref):
-        grad, sig = pad(p) * stage[strided(q), :], sig_ref[p]
-        grad_v = grad * sig
-        grad_e[:size, lanes(p)] = grad_v.astype(BF16)
-        grad_e[size:, lanes(p)] = (grad_v * value_ref[p] * (1.0 - sig)).astype(BF16)
+        grad = stage[strided(q), :]
+        grad_e[:size, lanes(p)] = (grad * sig_ref[p]).astype(BF16)
+        grad_e[size:, lanes(p)] = (grad * value_ref[p]).astype(BF16)
 
     def left_back(p, q):
         edge_grads(p, q, left_v, left_s)

time: 102 us -> 102 us (level)
  no operation moved by 1% of the time
where the time goes in v7:
time: 102 us
  Pallas kernels  101 us (99%)
    pallas_call x1, Pallas kernels, shards(): pl.pallas_call(functools.partial(kernel, rows, cols), out_shape=(pltpu.VM...  100 us

profile of v7, /device:TPU:1, one launch (start us, length us, event | category | flops | bytes accessed | tf_op | source)
XLA Modules:
  0.0 101.7 jit_solution(7685527932779054417)
XLA Ops:
  0.6 100.0 %triangle.1 = (bf16[32,64,128]{2,1,0:T(8,128)(2,1)S(1)}, bf16[32,64,128]{2,1,0:T(8,128)(2,1)S(1)}, f32[6,16,8,128]{3,2,1,0:T(8,128)S(1)}) custom-call(bf16[32,64,128]{2,1,0:T(8,128)(2,1)} %pair_in.1, bf16[32,64,128]{2,1,0:T(8,128)(2,1)} %cot_in.1, s32[512]{0:T(512)} %pad_in.1, s32[512]{0:T(512)} %crop_in.1, bf16[128,128]{1,0:T(8,128)(2,1)} %left_proj_in.1, ...), custom_call_target="tpu_custom_call" | custom-call | tf_op jit(solution)/shard_map/triangle/pallas_call | solution.py:588
  100.6 1.1 %settle.1 = (bf16[32,64,128]{2,1,0:T(8,128)(2,1)}, bf16[32,64,128]{2,1,0:T(8,128)(2,1)}, f32[6,16,8,128]{3,2,1,0:T(8,128)}) custom-call(bf16[32,64,128]{2,1,0:T(8,128)(2,1)S(1)} %get-tuple-element.9.refs_0_, bf16[32,64,128]{2,1,0:T(8,128)(2,1)S(1)} %get-tuple-element.10.refs_1_, f32[6,16,8,128]{3,2,1,0:T(8,128)S(1)} %get-tuple-element.11.refs_2_), custom_call_target="tpu_custom_call" | custom-call | tf_op jit(solution)/shard_map/settle/pallas_call | solution.py:540
